TPU v7x, 32 devices: a whole 2x2x4 slice. The times are simulated.
32 devices in a mesh: dp: 4 (over z), tm: 4 (over y, x), space: 2 (over core).
Axes of the slice: x: 2, y: 2, z: 4, core: 2. Of those that a mesh axis runs over, the one named last changes fastest.
Arguments:
- frames: bfloat16 [4, 32, 4, 16, 512], P('dp', 'tm', 'space'), may hold values from -6 to 6
- clip_ids: int32 [4, 16], P('dp', 'tm'), may hold values from 0 to 3, never falling along the last dimension, each value on 1 to 8 neighbouring positions
- kernel: bfloat16 [3, 3, 3, 512, 512], replicated, may hold values from -0.0546875 to 0.0546875
- cotangent: bfloat16 [4, 16, 4, 16, 512], P('dp', 'tm', 'space'), may hold values from -6 to 6
Outputs:
- activated: bfloat16 [4, 16, 4, 16, 512], P('dp', 'tm', 'space')
- frame_grad: bfloat16 [4, 32, 4, 16, 512], P('dp', 'tm', 'space')
- kernel_grad: float32 [27, 262144], P(None, ('dp', 'tm', 'space'))
Inputs may be any that keep to these rules, and one draw needn't show every extreme that they name: `clip_ids`: along each group's frame pairs the clip number never falls and starts at 0; each group holds 4 clips of 1 to 8 pairs, one of exactly 8 pairs.
All inputs are finite; a program needn't handle non-finite values.
Results may differ from a plain program's by a relative error of at most 0.0049.
Values may be sent and summed in bfloat16 or wider, within the bound.
A program may use at most 256 MiB of HBM per device.

v0:
```python
import jax
import jax.numpy as jnp
from jax import lax
from jax.sharding import PartitionSpec as P


def padded(array, sides, width):
    for axis, dim in sides:
        size, length = (lax.axis_size(axis), array.shape[dim])
        up = [(i, (i + 1) % size) for i in range(size - 1)]
        down = [(j, i) for i, j in up]
        last = lax.slice_in_dim(array, length - width, length, axis=dim)
        initial = lax.slice_in_dim(array, 0, width, axis=dim)
        before = lax.ppermute(last, axis, up)
        after = lax.ppermute(initial, axis, down)
        array = jnp.concatenate([before, array, after], axis=dim)
    return array


def from_behind(value, axis, steps):
    count = lax.axis_size(axis)
    initial, last = (max(0, -steps), min(count, count - steps))
    return lax.ppermute(value, axis, [(source, source + steps) for source in range(initial, last)])


def widen_columns(field):
    return jnp.pad(field, ((0, 0), (0, 0), (0, 0), (1, 1), (0, 0)))


def per_device(frames, clip_ids, kernel, cotangent):
    pair_count = clip_ids.shape[1]
    height = frames.shape[2]
    columns = frames.shape[3]
    channels = frames.shape[4]
    cell_count = pair_count * height * columns
    rowed = padded(frames, (("space", 2),), 1)
    earlier, prior_id = from_behind((rowed[:, -2:], clip_ids[:, -1:]), "tm", 1)
    extended = widen_columns(jnp.concatenate([earlier, rowed], axis=1))
    linked = (jnp.concatenate([prior_id, clip_ids[:, :-1]], axis=1) == clip_ids).astype(
        jnp.bfloat16
    )
    linked = linked[:, :, None, None, None]
    preact = jnp.zeros((cell_count, channels), jnp.float32)
    patches = []
    for time_tap in range(3):
        source = extended[:, time_tap : time_tap + 2 * pair_count : 2]
        if time_tap < 2:
            source = source * linked
        for row_tap in range(3):
            row_band = source[:, :, row_tap : row_tap + height]
            block = jnp.concatenate(
                [row_band[:, :, :, col_tap : col_tap + columns] for col_tap in range(3)], axis=-1
            ).reshape(cell_count, 3 * channels)
            patches.append(block)
            preact = preact + jnp.dot(
                block,
                kernel[time_tap, row_tap].reshape(3 * channels, channels),
                preferred_element_type=jnp.float32,
            )
    gating = jax.nn.sigmoid(preact)
    grid_shape = (frames.shape[0], pair_count, height, columns, channels)
    activated = (preact * gating).astype(jnp.bfloat16).reshape(grid_shape)
    upstream = (
        cotangent.reshape(cell_count, channels).astype(jnp.float32)
        * (gating * (1.0 + preact * (1.0 - gating)))
    ).astype(jnp.bfloat16)
    blocks = [
        lax.dot_general(
            block, upstream, (((0,), (0,)), ((), ())), preferred_element_type=jnp.float32
        )
        for block in patches
    ]
    term = jnp.concatenate(blocks, axis=0).reshape(27, channels * channels)
    kernel_grad = lax.psum_scatter(term, ("dp", "tm", "space"), scatter_dimension=1, tiled=True)
    grid = upstream.reshape(grid_shape)
    padded_rows = padded(grid, (("space", 2),), 1)
    later, next_id = from_behind((padded_rows[:, :1], clip_ids[:, :1]), "tm", -1)
    following = jnp.concatenate([padded_rows[:, 1:], later], axis=1)
    onward = (jnp.concatenate([clip_ids[:, 1:], next_id], axis=1) == clip_ids).astype(jnp.bfloat16)
    following = widen_columns(following * onward[:, :, None, None, None])
    current = widen_columns(padded_rows)

    def transpose_conv(field, time_tap):
        total = jnp.zeros((cell_count, channels), jnp.float32)
        for row_tap in range(3):
            row_band = field[:, :, 2 - row_tap : 2 - row_tap + height]
            stacked = jnp.stack(
                [row_band[:, :, :, 2 - col_tap : 2 - col_tap + columns] for col_tap in range(3)],
                axis=-2,
            ).reshape(cell_count, 3, channels)
            total = total + lax.dot_general(
                stacked,
                kernel[time_tap, row_tap],
                (((1, 2), (0, 2)), ((), ())),
                preferred_element_type=jnp.float32,
            )
        return total

    even_grad = transpose_conv(current, 2) + transpose_conv(following, 0)
    odd_grad = transpose_conv(following, 1)
    frame_grad = jnp.stack([even_grad.reshape(grid_shape), odd_grad.reshape(grid_shape)], axis=2)
    frame_grad = frame_grad.reshape(frames.shape).astype(jnp.bfloat16)
    return (activated, frame_grad, kernel_grad)


def solution(mesh):
    return jax.shard_map(
        per_device,
        mesh=mesh,
        in_specs=(
            P("dp", "tm", "space", None, None),
            P("dp", "tm"),
            P(),
            P("dp", "tm", "space", None, None),
        ),
        out_specs=(
            P("dp", "tm", "space", None, None),
            P("dp", "tm", "space", None, None),
            P(None, ("dp", "tm", "space")),
        ),
        check_vma=False,
    )
```

profile of v0, /device:TPU:11, one launch (start us, length us, event | category | flops | bytes accessed | tf_op | source)
XLA Modules:
  0.0 458.4 jit_solution(6400612718657904740)
XLA Ops:
  9.5 3.0 collective-permute-start.1
  13.9 3.1 collective-permute-start.3
  17.0 2.8 collective-permute-start.7
  19.8 5.9 %fusion.112 = (bf16[1,1,3,512,512]{4,3,2,1,0:T(8,128)(2,1)S(1)}, bf16[1,1,3,512,512]{4,3,2,1,0:T(8,128)(2,1)S(1)}, bf16[1,1,3,512,512]{4,3,2,1,0:T(8,128)(2,1)S(...) fusion(bf16[3,3,3,512,512]{4,3,2,1,0:T(8,128)(2,1)} %param.6), kind=kLoop, calls=%fused_computation.134 | loop fusion | bytes 28311552 | tf_op jit(solution)/shard_map/slice | solution.py:57
  25.9 3.5 collective-permute-start.2
  30.8 2.2 collective-permute-done.2
  39.0 2.2 convolution_dynamic-update-slice_fusion.8
  41.3 2.3 convolution_dynamic-update-slice_fusion.7
  43.5 2.2 convolution_dynamic-update-slice_fusion.6
  45.8 2.2 convolution_dynamic-update-slice_fusion.5
  48.0 2.2 convolution_dynamic-update-slice_fusion.4
  50.2 2.2 convolution_dynamic-update-slice_fusion.3
  52.4 2.3 convolution_dynamic-update-slice_fusion.2
  54.7 2.3 convolution_dynamic-update-slice_fusion.1
  57.0 2.3 convolution_dynamic-update-slice_fusion
  59.2 31.0 %reshape.152 = f32[27,262144]{1,0:T(8,128)} reshape(f32[13824,512]{1,0:T(8,128)} %convolution_dynamic-update-slice_fusion) | data formatting | bytes 56623104 | tf_op jit(solution)/shard_map/reshape | solution.py:73
  91.5 3.0 collective-permute-start.5
  95.5 2.1 collective-permute-start.6
  97.8 2.5 fusion.21
  104.7 2.1 fusion.30
  110.9 2.1 fusion.72
  113.0 2.1 fusion.60
  115.1 2.1 fusion.69
  118.0 333.5 %reduce-scatter.2.cloned.1.call-done = f32[27,8192]{1,0:T(8,128)} async-done(((f32[27,262144]{1,0:T(8,128)}), f32[27,8192]{1,0:T(8,128)}) %reduce-scatter.2.cloned.1.call-update) | async-done | bytes 884752 | tf_op jit(solution)/shard_map/reduce_scatter | solution.py:74
  (60 shorter events, 22.6 us)
Async XLA Ops:
  7.2 444.4 %reduce-scatter.2.cloned.1.call-start = ((), (), s32[]{:S(2)}) async-start(), calls=%async_computation.1 | async-start | bytes 34603008 | tf_op jit(solution)/shard_map/reduce_scatter | solution.py:74
  8.2 17.6 %collective-permute-start = (bf16[1,8,1,16,512]{4,3,2,1,0:T(8,128)(2,1)S(1)}, bf16[1,8,1,16,512]{4,3,2,1,0:T(8,128)(2,1)S(1)}, u32[]{:S(2)}, u32[]{:S(2)}) collective-permute-start(bf16[1,8,1,16,512]{4,3,2,1,0:T(8,128)(2,1)S(1)} %get-tuple-element.60), channel_id=1, source_target_pairs={{0,1},{2,3},{4,5},{6,7},{8,9},{10,11},{12,13},{14,15},{16,17},{18,... | collective-permute-start | bytes 393224 | tf_op jit(solution)/shard_map/ppermute | solution.py:14
  9.5 16.4 %collective-permute-start.1 = (bf16[1,8,1,16,512]{4,3,2,1,0:T(8,128)(2,1)S(1)}, bf16[1,8,1,16,512]{4,3,2,1,0:T(8,128)(2,1)S(1)}, u32[]{:S(2)}, u32[]{:S(2)}) collective-permute-start(bf16[1,8,1,16,512]{4,3,2,1,0:T(8,128)(2,1)S(1)} %get-tuple-element.59), channel_id=1, source_target_pairs={{1,0},{3,2},{5,4},{7,6},{9,8},{11,10},{13,12},{15,14},{17,16},{19,... | collective-permute-start | bytes 393224 | tf_op jit(solution)/shard_map/ppermute | solution.py:15
  13.9 15.6 %collective-permute-start.3 = (s32[1,1]{1,0:T(1,128)}, s32[1,1]{1,0:T(1,128)}, u32[]{:S(2)}, u32[]{:S(2)}) collective-permute-start(s32[1,1]{1,0:T(1,128)} %get-tuple-element.70), channel_id=1, source_target_pairs={{0,2},{2,4},{4,6},{1,3},{3,5},{5,7},{8,10},{10,12},{12,14},{9,11},... | collective-permute-start | bytes 20 | tf_op jit(solution)/shard_map/ppermute | solution.py:23
  17.0 8.8 %copy-start.1 = (s32[1,4]{1,0:T(1,128)S(1)}, s32[1,4]{1,0:T(1,128)}, u32[]{:S(2)}) copy-start(s32[1,4]{1,0:T(1,128)} %param.5) | copy-start | bytes 52
  17.0 8.8 %copy-start = (bf16[1,8,2,16,512]{4,3,2,1,0:T(8,128)(2,1)S(1)}, bf16[1,8,2,16,512]{4,3,2,1,0:T(8,128)(2,1)}, u32[]{:S(2)}) copy-start(bf16[1,8,2,16,512]{4,3,2,1,0:T(8,128)(2,1)} %param.4) | copy-start | bytes 786436
  17.0 12.5 %collective-permute-start.7 = (s32[1,1]{1,0:T(1,128)}, s32[1,1]{1,0:T(1,128)}, u32[]{:S(2)}, u32[]{:S(2)}) collective-permute-start(s32[1,1]{1,0:T(1,128)} %get-tuple-element.69), channel_id=1, source_target_pairs={{2,0},{4,2},{6,4},{3,1},{5,3},{7,5},{10,8},{12,10},{14,12},{11,9},... | collective-permute-start | bytes 20 | tf_op jit(solution)/shard_map/ppermute | solution.py:23
  25.9 7.1 %collective-permute-start.2 = (bf16[1,2,4,16,512]{4,3,2,1,0:T(8,128)(2,1)S(1)}, bf16[1,2,4,16,512]{4,3,2,1,0:T(8,128)(2,1)S(1)}, u32[]{:S(2)}, u32[]{:S(2)}) collective-permute-start(bf16[1,2,4,16,512]{4,3,2,1,0:T(8,128)(2,1)S(1)} %slice.358), channel_id=1, source_target_pairs={{0,2},{2,4},{4,6},{1,3},{3,5},{5,7},{8,10},{10,12},{12,14},{9,11},... | collective-permute-start | bytes 393224 | tf_op jit(solution)/shard_map/ppermute | solution.py:23
  37.0 0.9 copy-start.2
  90.2 4.3 collective-permute-start.4
  91.5 3.9 collective-permute-start.5
  95.5 9.0 %collective-permute-start.6 = (bf16[1,1,4,16,512]{4,3,2,1,0:T(8,128)(2,1)S(1)}, bf16[1,1,4,16,512]{4,3,2,1,0:T(8,128)(2,1)S(1)}, u32[]{:S(2)}, u32[]{:S(2)}) collective-permute-start(bf16[1,1,4,16,512]{4,3,2,1,0:T(8,128)(2,1)S(1)} %slice.389), channel_id=1, source_target_pairs={{2,0},{4,2},{6,4},{3,1},{5,3},{7,5},{10,8},{12,10},{14,12},{11,9},... | collective-permute-start | bytes 196616 | tf_op jit(solution)/shard_map/ppermute | solution.py:23
Sparse Core Ops, SparseCore 0:
  90.3 361.1 reduce-scatter.1
where the time goes:
time: 462 us; the launch traced here: 458 us
  waiting for transfers between devices  337 us (73%)
  matrix products  43.4 us (9%)
  local copies, waits for them, and re-layouts  41.3 us (9%)
  starting transfers between devices  20.2 us (4%)
  between operations  14.5 us (3%)
    reduce_scatter x1, waiting for transfers between devices, per_device(): lax.psum_scatter(term, ('dp', 'tm', 'space'), scatter_dimension=1, tiled=...  334 us
    reshape x1, local copies, waits for them, and re-layouts, per_device(): term = jnp.concatenate(blocks, axis=0).reshape(27, channels * channels)  31 us
    dot_general x9, matrix products, per_device(): lax.dot_general(block, upstream, (((0,), (0,)), ((), ())), preferred_elem...  20.2 us
    dot_general x9, matrix products, transpose_conv(): lax.dot_general(stacked, kernel[time_tap, row_tap], (((1, 2), (0, 2)), ((...  19.1 us
    ppermute x4, starting transfers between devices, from_behind(): lax.ppermute(value, axis, [(source, source + steps) for source in range(i...  11.5 us
  transfers between devices with their start and end apart: 9, of which 3 were waited for; matrix products, arithmetic and copies ran while one was open for 6% of the time, Pallas kernels for 0%

commit v1 on v0

v1 whole, which is shorter than its diff:
```python
import functools

import jax
import jax.numpy as jnp
from jax import lax
from jax.experimental import pallas as pl
from jax.experimental.pallas import tpu as pltpu
from jax.sharding import PartitionSpec as P

AXES = ("dp", "tm", "space")
VMEM_BYTES = 48 * 2**20


def row_halo(array):
    size = lax.axis_size("space")
    up = [(i, i + 1) for i in range(size - 1)]
    down = [(i + 1, i) for i in range(size - 1)]
    before = lax.ppermute(array[:, :, -1:], "space", up)
    after = lax.ppermute(array[:, :, :1], "space", down)
    return jnp.concatenate([before, array, after], axis=2)


def from_behind(value, steps):
    count = lax.axis_size("tm")
    first, last = max(0, -steps), min(count, count - steps)
    return lax.ppermute(value, "tm", [(i, i + steps) for i in range(first, last)])


def column_taps(base, columns):
    count = base.shape[0]
    wide = base.astype(jnp.float32)
    column = lax.broadcasted_iota(jnp.int32, base.shape, 0) % columns
    left = jnp.where(column > 0, pltpu.roll(wide, 1, 0), 0.0)
    right = jnp.where(column < columns - 1, pltpu.roll(wide, count - 1, 0), 0.0)
    return left.astype(base.dtype), base, right.astype(base.dtype)


def forward_body(columns, height, planes, weights, cotangent, activated, upstream, total):
    step = pl.program_id(0)
    time_tap, row_tap = step // 3, step % 3
    pairs, channels = planes.shape[1], planes.shape[-1]
    base = planes[time_tap, :, pl.ds(row_tap, height)].reshape(pairs * height * columns, channels)
    block = jnp.concatenate(column_taps(base, columns), axis=1)
    term = jnp.dot(
        block,
        weights[0, 0].reshape(3 * channels, channels),
        preferred_element_type=jnp.float32,
    )

    @pl.when(step == 0)
    def _():
        total[...] = term

    @pl.when(step > 0)
    def _():
        total[...] += term

    @pl.when(step == 8)
    def _():
        preact = total[...]
        gating = jax.nn.sigmoid(preact)
        activated[...] = (preact * gating).astype(activated.dtype)
        slope = gating * (1.0 + preact * (1.0 - gating))
        upstream[...] = (cotangent[...].astype(jnp.float32) * slope).astype(upstream.dtype)


def backward_body(columns, height, fields, weights, out, total):
    step = pl.program_id(0)
    place, row_tap = step // 3, step % 3
    pairs, channels = fields.shape[1], fields.shape[-1]
    source = jnp.where(place == 1, 1, 0)
    base = fields[source, :, pl.ds(2 - row_tap, height)].reshape(
        pairs * height * columns, channels
    )
    left, middle, right = column_taps(base, columns)
    term = None
    for col_tap, part in enumerate((right, middle, left)):
        product = lax.dot_general(
            part,
            weights[0, 0, col_tap],
            (((1,), (1,)), ((), ())),
            preferred_element_type=jnp.float32,
        )
        term = product if term is None else term + product
    fresh = (step == 0) | (step == 6)

    @pl.when(fresh)
    def _():
        total[...] = term

    @pl.when(jnp.logical_not(fresh))
    def _():
        total[...] += term

    def store(parity):
        value = total[...].astype(out.dtype)
        out[:, parity] = value.reshape(pairs, height * columns, channels)

    @pl.when(step == 5)
    def _():
        store(0)

    @pl.when(step == 8)
    def _():
        store(1)


def weight_body(columns, rows, planes, upstream, out):
    cells = planes.shape[-1]
    own = planes.shape[-2]
    lane = lax.broadcasted_iota(jnp.int32, (own, cells), 1)
    column = lane % columns
    row = (lane // columns) % rows
    frame = rows * columns
    parts = []
    for time_tap in range(3):
        plane = planes[0, 0, time_tap].astype(jnp.float32)
        if time_tap < 2:
            plane = jnp.where(lane >= frame, pltpu.roll(plane, frame, 1), 0.0)
        for down in (-1, 0, 1):
            for right in (-1, 0, 1):
                shift = down * columns + right
                moved = pltpu.roll(plane, (-shift) % cells, 1) if shift else plane
                inside = (row + down >= 0) & (row + down < rows)
                inside = inside & (column + right >= 0) & (column + right < columns)
                parts.append(jnp.where(inside, moved, 0.0))
    patches = jnp.concatenate(parts, axis=0).astype(jnp.bfloat16)
    _, tm, space, _, pairs, _, _ = upstream.shape
    field = jnp.concatenate(
        [upstream[0, t, s, 0, p] for t in range(tm) for p in range(pairs) for s in range(space)],
        axis=0,
    )
    term = jnp.dot(patches, field, preferred_element_type=jnp.float32)
    first = (pl.program_id(0) == 0) & (pl.program_id(1) == 0)

    @pl.when(first)
    def _():
        out[...] = term

    @pl.when(jnp.logical_not(first))
    def _():
        out[...] += term


def per_device(frames, clip_ids, kernel, cotangent):
    dp, tm, space = (lax.axis_size(axis) for axis in AXES)
    groups, steps, height, columns, channels = frames.shape
    pairs = clip_ids.shape[1]
    slots = groups * pairs
    frame = height * columns
    cells = slots * frame
    own = channels // (dp * tm * space)
    bf16 = jnp.bfloat16

    next_id = from_behind(clip_ids[:, :1], -1)
    prior_id = from_behind(clip_ids[:, -1:], 1)
    linked = (jnp.concatenate([prior_id, clip_ids[:, :-1]], axis=1) == clip_ids).astype(bf16)
    onward = (jnp.concatenate([clip_ids[:, 1:], next_id], axis=1) == clip_ids).astype(bf16)

    paired = frames.reshape(slots, 2, frame, channels)
    kept = onward.reshape(slots, 1, 1)
    even, odd = paired[:, 0], paired[:, 1]
    planes = jnp.stack([even * kept, odd * kept, even], axis=0).reshape(3 * cells, channels)
    sent = planes.T.reshape(dp * tm * space, own, 3 * cells)
    got = lax.all_to_all(sent, AXES, 0, 0)
    got = got.reshape(dp, tm, space, own, 3, groups, pairs, frame)
    own_planes = got.transpose(0, 5, 4, 3, 1, 6, 2, 7).reshape(dp, groups, 3, own, -1)

    rowed = row_halo(frames)
    earlier = from_behind(rowed[:, -2:], 1)
    extended = jnp.concatenate([earlier, rowed], axis=1)
    gate = linked[:, :, None, None, None]
    taps = jnp.stack(
        [
            extended[:, 0 : 2 * pairs : 2] * gate,
            extended[:, 1 : 1 + 2 * pairs : 2] * gate,
            extended[:, 2 : 2 + 2 * pairs : 2],
        ],
        axis=0,
    ).reshape(3, slots, height + 2, columns, channels)

    whole = pl.BlockSpec(memory_space=pltpu.VMEM)
    params = pltpu.CompilerParams(vmem_limit_bytes=VMEM_BYTES)
    flops = 2 * 27 * cells * channels * channels
    weight_bytes = 27 * channels * channels * 2
    cost = pl.CostEstimate(flops=flops, bytes_accessed=weight_bytes, transcendentals=0)
    flat = jax.ShapeDtypeStruct((cells, channels), bf16)
    activated, upstream = pl.pallas_call(
        functools.partial(forward_body, columns, height),
        grid=(9,),
        out_shape=(flat, flat),
        in_specs=[
            whole,
            pl.BlockSpec((1, 1, 3, channels, channels), lambda i: (i // 3, i % 3, 0, 0, 0)),
            whole,
        ],
        out_specs=(
            pl.BlockSpec((cells, channels), lambda i: (0, 0)),
            pl.BlockSpec((cells, channels), lambda i: (0, 0)),
        ),
        scratch_shapes=[pltpu.VMEM((cells, channels), jnp.float32)],
        compiler_params=params,
        cost_estimate=cost,
    )(taps, kernel, cotangent.reshape(cells, channels))

    gathered = lax.all_gather(upstream, AXES, axis=0, tiled=True)

    grid = upstream.reshape(groups, pairs, height, columns, channels)
    padded = row_halo(grid)
    later = from_behind(padded[:, :1], -1)
    following = jnp.concatenate([padded[:, 1:], later], axis=1)
    following = following * onward[:, :, None, None, None]
    fields = jnp.stack([following, padded], axis=0).reshape(
        2, slots, height + 2, columns, channels
    )
    frame_grad = pl.pallas_call(
        functools.partial(backward_body, columns, height),
        grid=(9,),
        out_shape=jax.ShapeDtypeStruct((slots, 2, frame, channels), bf16),
        in_specs=[
            whole,
            pl.BlockSpec(
                (1, 1, 3, channels, channels), lambda i: ((i // 3) * 2 % 3, i % 3, 0, 0, 0)
            ),
        ],
        out_specs=pl.BlockSpec((slots, 2, frame, channels), lambda i: (0, 0, 0, 0)),
        scratch_shapes=[pltpu.VMEM((cells, channels), jnp.float32)],
        compiler_params=params,
        cost_estimate=cost,
    )(fields, kernel)

    per_group = gathered.reshape(dp, tm, space, groups, pairs, frame, channels)
    group_cells = tm * pairs * space * frame
    kernel_grad = pl.pallas_call(
        functools.partial(weight_body, columns, space * height),
        grid=(dp, groups),
        out_shape=jax.ShapeDtypeStruct((27 * own, channels), jnp.float32),
        in_specs=[
            pl.BlockSpec((1, 1, 3, own, group_cells), lambda a, b: (a, b, 0, 0, 0)),
            pl.BlockSpec(
                (1, tm, space, 1, pairs, frame, channels), lambda a, b: (a, 0, 0, b, 0, 0, 0)
            ),
        ],
        out_specs=pl.BlockSpec((27 * own, channels), lambda a, b: (0, 0)),
        compiler_params=params,
        cost_estimate=pl.CostEstimate(
            flops=flops, bytes_accessed=2 * gathered.size, transcendentals=0
        ),
    )(own_planes, per_group)

    return (
        activated.reshape(cotangent.shape),
        frame_grad.reshape(frames.shape),
        kernel_grad.reshape(27, own * channels),
    )


def solution(mesh):
    return jax.shard_map(
        per_device,
        mesh=mesh,
        in_specs=(
            P("dp", "tm", "space", None, None),
            P("dp", "tm"),
            P(),
            P("dp", "tm", "space", None, None),
        ),
        out_specs=(
            P("dp", "tm", "space", None, None),
            P("dp", "tm", "space", None, None),
            P(None, ("dp", "tm", "space")),
        ),
        check_vma=False,
    )
```

time: 462 us -> 124 us (0.27)
  waiting for transfers between devices: 337 us -> 34.7 us
  matrix products: 43.4 us -> 0 us
  local copies, waits for them, and re-layouts: 41.3 us -> 14.3 us
  Pallas kernels: 0 us -> 25.4 us
  starting transfers between devices: 20.2 us -> 29.8 us
    reduce_scatter x1 -> x0, waiting for transfers between devices: 334 us -> none  [per_device(): lax.psum_scatter(term, ('dp', 'tm', 'space'), scatter_dimension=1, tiled=...]
    dot_general x27 -> x0, matrix products: 43.4 us -> none  [the longest x9 20.2 us: per_device(): lax.dot_general(block, upstream, (((0,), (0,)), ((), ())), preferred_elem...]
    reshape x1 -> x3, local copies, waits for them, and re-layouts: 31 us -> 3.69 us  [the longest x1 1.6 us: per_device(): got.transpose(0, 5, 4, 3, 1, 6, 2, 7).reshape(dp, groups, 3, own, -1)]
    all_gather x0 -> x1, waiting for transfers between devices: none -> 26.6 us  [per_device(): gathered = lax.all_gather(upstream, AXES, axis=0, tiled=True)]
    pallas_call x0 -> x3, Pallas kernels: none -> 25.4 us  [the longest x1 11.4 us: per_device(): pl.pallas_call(functools.partial(backward_body, columns, height), grid=(9...]
    all_to_all x0 -> x1, starting transfers between devices: none -> 7.74 us  [per_device(): got = lax.all_to_all(sent, AXES, 0, 0)]
    slice x11 -> x5, local copies, waits for them, and re-layouts: 9.07 us -> 3.24 us  [the longest x1 1.31 us: per_device(): next_id = from_behind(clip_ids[:, :1], -1)]
    ppermute x8, waiting for transfers between devices: 3.07 us -> 8.05 us  [the longest x4 8.04 us: from_behind(): lax.ppermute(value, 'tm', [(i, i + steps) for i in range(first, last)])]
  transfers between devices with their start and end apart: 9 -> 10, of which waited for: 3 -> 3; matrix products, arithmetic and copies ran while one was open for 6% -> 11% of each run, Pallas kernels for 0% -> 9%
where the time goes in v1:
time: 124 us; the launch traced here: 122 us
  waiting for transfers between devices  34.7 us (28%)
  starting transfers between devices  29.8 us (24%)
  Pallas kernels  25.4 us (20%)
  local copies, waits for them, and re-layouts  14.3 us (12%)
  between operations  14.3 us (12%)
  other arithmetic  3.52 us (3%)
    all_gather x1, waiting for transfers between devices, per_device(): gathered = lax.all_gather(upstream, AXES, axis=0, tiled=True)  26.6 us
    ppermute x4, starting transfers between devices, from_behind(): lax.ppermute(value, 'tm', [(i, i + steps) for i in range(first, last)])  12.9 us
    pallas_call x1, Pallas kernels, per_device(): pl.pallas_call(functools.partial(backward_body, columns, height), grid=(9...  11.4 us
    pallas_call x1, Pallas kernels, per_device(): pl.pallas_call(functools.partial(forward_body, columns, height), grid=(9,...  10.2 us
    ppermute x4, waiting for transfers between devices, from_behind(): lax.ppermute(value, 'tm', [(i, i + steps) for i in range(first, last)])  8.04 us
    all_to_all x1, starting transfers between devices, per_device(): got = lax.all_to_all(sent, AXES, 0, 0)  7.74 us
    ppermute x2, starting transfers between devices, row_halo(): after = lax.ppermute(array[:, :, :1], 'space', down)  6.47 us
    pallas_call x1, Pallas kernels, per_device(): pl.pallas_call(functools.partial(weight_body, columns, space * height), g...  3.73 us
  transfers between devices with their start and end apart: 10, of which 3 were waited for; matrix products, arithmetic and copies ran while one was open for 11% of the time, Pallas kernels for 9%

profile of v1, /device:TPU:11, one launch (start us, length us, event | category | flops | bytes accessed | tf_op | source)
XLA Modules:
  0.0 121.9 jit_solution(6825084926042188455)
XLA Ops:
  7.2 1.0 fusion.5
  8.2 1.3 %collective-permute-start = (bf16[1,8,1,16,512]{4,3,2,1,0:T(8,128)(2,1)S(1)}, bf16[1,8,1,16,512]{4,3,2,1,0:T(8,128)(2,1)S(1)}, u32[]{:S(2)}, u32[]{:S(2)}) collective-permute-start(bf16[1,8,1,16,512]{4,3,2,1,0:T(8,128)(2,1)S(1)} %get-tuple-element.14), channel_id=1, source_target_pairs={{0,1},{2,3},{4,5},{6,7},{8,9},{10,11},{12,13},{14,15},{16,17},{18,... | collective-permute-start | bytes 393224 | tf_op jit(solution)/shard_map/ppermute | solution.py:18
  9.5 3.0 %collective-permute-start.1 = (bf16[1,8,1,16,512]{4,3,2,1,0:T(8,128)(2,1)S(1)}, bf16[1,8,1,16,512]{4,3,2,1,0:T(8,128)(2,1)S(1)}, u32[]{:S(2)}, u32[]{:S(2)}) collective-permute-start(bf16[1,8,1,16,512]{4,3,2,1,0:T(8,128)(2,1)S(1)} %get-tuple-element.13), channel_id=1, source_target_pairs={{1,0},{3,2},{5,4},{7,6},{9,8},{11,10},{13,12},{15,14},{17,16},{19,... | collective-permute-start | bytes 393224 | tf_op jit(solution)/shard_map/ppermute | solution.py:19
  12.6 1.3 %fusion.8 = (s32[1,1]{1,0:T(1,128)}, s32[1,1]{1,0:T(1,128)}) fusion(s32[1,4]{1,0:T(1,128)} %param.5), kind=kLoop, calls=%fused_computation.26 | loop fusion | bytes 16 | tf_op jit(solution)/shard_map/slice | solution.py:155
  13.9 2.2 %collective-permute-start.7 = (s32[1,1]{1,0:T(1,128)}, s32[1,1]{1,0:T(1,128)}, u32[]{:S(2)}, u32[]{:S(2)}) collective-permute-start(s32[1,1]{1,0:T(1,128)} %get-tuple-element.21), channel_id=1, source_target_pairs={{2,0},{4,2},{6,4},{3,1},{5,3},{7,5},{10,8},{12,10},{14,12},{11,9},... | collective-permute-start | bytes 20 | tf_op jit(solution)/shard_map/ppermute | solution.py:26
  16.1 4.0 %collective-permute-start.3 = (s32[1,1]{1,0:T(1,128)}, s32[1,1]{1,0:T(1,128)}, u32[]{:S(2)}, u32[]{:S(2)}) collective-permute-start(s32[1,1]{1,0:T(1,128)} %get-tuple-element.22), channel_id=1, source_target_pairs={{0,2},{2,4},{4,6},{1,3},{3,5},{5,7},{8,10},{10,12},{12,14},{9,11},... | collective-permute-start | bytes 20 | tf_op jit(solution)/shard_map/ppermute | solution.py:26
  20.9 2.0 %fusion.3 = (bf16[4]{0:T(256)(128)(2,1)S(1)}, bf16[4]{0:T(256)(128)(2,1)S(1)}) fusion(s32[1,4]{1,0:T(1,128)} %param.5, s32[1,1]{1,0:T(1,128)} %collective-permute-done.7, s32[1,3]{1,0:T(1,128)S(1)} %get-tuple-element.19, s32[1,3]{1,0:T(1,128)S(1)} %get-tuple-element.20, s32[1,1]{1,0:T(1,128)} %collective-permute-done.3), kind=kLoop, calls=%fused_computation.21 | loop fusion | flops 24 | bytes 64 | tf_op jit(solution)/shard_map/mul | solution.py:212
  23.0 1.0 constant_dynamic-update-slice_fusion.1
  24.0 4.6 %collective-permute-start.2 = (bf16[1,2,4,16,512]{4,3,2,1,0:T(8,128)(2,1)S(1)}, bf16[1,2,4,16,512]{4,3,2,1,0:T(8,128)(2,1)S(1)}, u32[]{:S(2)}, u32[]{:S(2)}) collective-permute-start(bf16[1,2,4,16,512]{4,3,2,1,0:T(8,128)(2,1)S(1)} %slice.64), channel_id=1, source_target_pairs={{0,2},{2,4},{4,6},{1,3},{3,5},{5,7},{8,10},{10,12},{12,14},{9,11},... | collective-permute-start | bytes 393224 | tf_op jit(solution)/shard_map/ppermute | solution.py:26
  28.6 2.1 %collective-permute-done.2 = bf16[1,2,4,16,512]{4,3,2,1,0:T(8,128)(2,1)S(1)} collective-permute-done((bf16[1,2,4,16,512]{4,3,2,1,0:T(8,128)(2,1)S(1)}, bf16[1,2,4,16,512]{4,3,2,1,0:T(8,128)(2,1)S(1)}, u32[]{:S(2)}, u32[]{:S(2)}) %collective-permute-start.2) | collective-permute-done | bytes 131104 | tf_op jit(solution)/shard_map/ppermute | solution.py:26
  31.1 10.2 %shard_map.67 = (bf16[128,512]{1,0:T(8,128)(2,1)}, bf16[128,512]{1,0:T(8,128)(2,1)}) custom-call(bf16[3,4,4,16,512]{4,3,2,1,0:T(8,128)(2,1)S(1)} %maximum_bitcast_fusion.planes, bf16[3,3,3,512,512]{4,3,2,1,0:T(8,128)(2,1)} %weights.3, bf16[128,512]{1,0:T(8,128)(2,1)S(1)} %bitcast.48), custom_call_target="tpu_custom_call" | custom-call | flops 1811939328 | bytes 14155776 | tf_op jit(solution)/shard_map/pallas_call | solution.py:188
  42.3 3.4 %collective-permute-start.5 = (bf16[1,4,1,16,512]{4,3,2,1,0:T(8,128)(2,1)S(1)}, bf16[1,4,1,16,512]{4,3,2,1,0:T(8,128)(2,1)S(1)}, u32[]{:S(2)}, u32[]{:S(2)}) collective-permute-start(bf16[1,4,1,16,512]{4,3,2,1,0:T(8,128)(2,1)S(1)} %get-tuple-element.16), channel_id=1, source_target_pairs={{1,0},{3,2},{5,4},{7,6},{9,8},{11,10},{13,12},{15,14},{17,16},{19,... | collective-permute-start | bytes 196616 | tf_op jit(solution)/shard_map/ppermute | solution.py:19
  45.7 1.3 %collective-permute-start.4 = (bf16[1,4,1,16,512]{4,3,2,1,0:T(8,128)(2,1)S(1)}, bf16[1,4,1,16,512]{4,3,2,1,0:T(8,128)(2,1)S(1)}, u32[]{:S(2)}, u32[]{:S(2)}) collective-permute-start(bf16[1,4,1,16,512]{4,3,2,1,0:T(8,128)(2,1)S(1)} %get-tuple-element.15), channel_id=1, source_target_pairs={{0,1},{2,3},{4,5},{6,7},{8,9},{10,11},{12,13},{14,15},{16,17},{18,... | collective-permute-start | bytes 196616 | tf_op jit(solution)/shard_map/ppermute | solution.py:18
  48.0 7.7 %all-to-all-start = ((bf16[32,16,384]{2,1,0:T(8,128)(2,1)}), bf16[32,16,384]{2,1,0:T(8,128)(2,1)S(1)}, u32[]{:S(2)}, u32[]{:S(2)}) async-start(bf16[32,16,384]{2,1,0:T(8,128)(2,1)} %bitcast.22), calls=%async_computation | async-start | bytes 786432 | tf_op jit(solution)/shard_map/all_to_all | solution.py:165
  55.8 0.9 pad_maximum_fusion.2
  56.8 2.2 %collective-permute-start.6 = (bf16[1,1,4,16,512]{4,3,2,1,0:T(8,128)(2,1)S(1)}, bf16[1,1,4,16,512]{4,3,2,1,0:T(8,128)(2,1)S(1)}, u32[]{:S(2)}, u32[]{:S(2)}) collective-permute-start(bf16[1,1,4,16,512]{4,3,2,1,0:T(8,128)(2,1)S(1)} %slice.68), channel_id=1, source_target_pairs={{2,0},{4,2},{6,4},{3,1},{5,3},{7,5},{10,8},{12,10},{14,12},{11,9},... | collective-permute-start | bytes 196616 | tf_op jit(solution)/shard_map/ppermute | solution.py:26
  59.0 5.9 %collective-permute-done.6 = bf16[1,1,4,16,512]{4,3,2,1,0:T(8,128)(2,1)S(1)} collective-permute-done((bf16[1,1,4,16,512]{4,3,2,1,0:T(8,128)(2,1)S(1)}, bf16[1,1,4,16,512]{4,3,2,1,0:T(8,128)(2,1)S(1)}, u32[]{:S(2)}, u32[]{:S(2)}) %collective-permute-start.6) | collective-permute-done | bytes 65568 | tf_op jit(solution)/shard_map/ppermute | solution.py:26
  65.0 11.4 %shard_map.68 = bf16[4,2,32,512]{3,2,1,0:T(8,128)(2,1)} custom-call(bf16[2,4,4,16,512]{4,3,2,1,0:T(8,128)(2,1)S(1)} %maximum_bitcast_fusion.1.fields, bf16[3,3,3,512,512]{4,3,2,1,0:T(8,128)(2,1)} %weights.3), custom_call_target="tpu_custom_call" | custom-call | flops 1811939328 | bytes 14155776 | tf_op jit(solution)/shard_map/pallas_call | solution.py:216
  77.4 2.4 %copy.27 = bf16[4,1,3,16,4,4,2,32]{7,6,5,4,3,2,0,1:T(2,128)(2,1)S(1)} copy(bf16[4,1,3,16,4,4,2,32]{7,5,2,3,6,4,0,1:T(4,128)(2,1)S(1)} %bitcast.50) | data formatting | bytes 786432 | tf_op jit(solution)/shard_map/transpose | solution.py:167
  79.8 1.6 %reshape.123.planes = bf16[4,1,3,16,1024]{4,3,2,1,0:T(8,128)(2,1)S(1)} reshape(bf16[4,1,3,16,4,4,2,32]{7,6,5,4,3,2,0,1:T(2,128)(2,1)S(1)} %copy.27) | data formatting | bytes 786432 | tf_op jit(solution)/shard_map/reshape | solution.py:167
  81.4 26.6 %all-gather.2.cloned.1.call-done = bf16[4096,512]{1,0:T(8,128)(2,1)} async-done(((bf16[128,512]{1,0:T(8,128)(2,1)}), bf16[4096,512]{1,0:T(8,128)(2,1)}) %all-gather.2.cloned.1.call-update) | async-done | bytes 4194320 | tf_op jit(solution)/shard_map/all_gather | solution.py:206
  108.0 2.2 %copy-done.1 = bf16[4096,512]{1,0:T(8,128)(2,1)S(1)} copy-done((bf16[4096,512]{1,0:T(8,128)(2,1)S(1)}, bf16[4096,512]{1,0:T(8,128)(2,1)}, u32[]{:S(2)}) %copy-start.1) | copy-done | bytes 4194328
  110.2 3.7 %shard_map.69 = f32[432,512]{1,0:T(8,128)S(1)} custom-call(bf16[4,1,3,16,1024]{4,3,2,1,0:T(8,128)(2,1)S(1)} %reshape.123.planes, bf16[4,4,2,1,4,32,512]{6,5,4,3,2,1,0:T(8,128)(2,1)S(1)} %bitcast.49), custom_call_target="tpu_custom_call" | custom-call | flops 1811939328 | bytes 4194304 | tf_op jit(solution)/shard_map/pallas_call | solution.py:234
  113.9 1.2 reshape.125
  (32 shorter events, 4.3 us)
Async XLA Ops:
  7.2 23.9 %copy-start = (bf16[1,4,2,16,512]{4,3,2,1,0:T(8,128)(2,1)S(1)}, bf16[1,4,2,16,512]{4,3,2,1,0:T(8,128)(2,1)}, u32[]{:S(2)}) copy-start(bf16[1,4,2,16,512]{4,3,2,1,0:T(8,128)(2,1)} %param.7) | copy-start | bytes 393220
  7.2 100.8 %all-gather.2.cloned.1.call-start = ((), (), s32[]{:S(2)}) async-start(), calls=%async_computation.1 | async-start | bytes 4325376 | tf_op jit(solution)/shard_map/all_gather | solution.py:206
  8.2 14.7 %collective-permute-start = (bf16[1,8,1,16,512]{4,3,2,1,0:T(8,128)(2,1)S(1)}, bf16[1,8,1,16,512]{4,3,2,1,0:T(8,128)(2,1)S(1)}, u32[]{:S(2)}, u32[]{:S(2)}) collective-permute-start(bf16[1,8,1,16,512]{4,3,2,1,0:T(8,128)(2,1)S(1)} %get-tuple-element.14), channel_id=1, source_target_pairs={{0,1},{2,3},{4,5},{6,7},{8,9},{10,11},{12,13},{14,15},{16,17},{18,... | collective-permute-start | bytes 393224 | tf_op jit(solution)/shard_map/ppermute | solution.py:18
  9.5 14.4 %collective-permute-start.1 = (bf16[1,8,1,16,512]{4,3,2,1,0:T(8,128)(2,1)S(1)}, bf16[1,8,1,16,512]{4,3,2,1,0:T(8,128)(2,1)S(1)}, u32[]{:S(2)}, u32[]{:S(2)}) collective-permute-start(bf16[1,8,1,16,512]{4,3,2,1,0:T(8,128)(2,1)S(1)} %get-tuple-element.13), channel_id=1, source_target_pairs={{1,0},{3,2},{5,4},{7,6},{9,8},{11,10},{13,12},{15,14},{17,16},{19,... | collective-permute-start | bytes 393224 | tf_op jit(solution)/shard_map/ppermute | solution.py:19
  13.9 7.0 %collective-permute-start.7 = (s32[1,1]{1,0:T(1,128)}, s32[1,1]{1,0:T(1,128)}, u32[]{:S(2)}, u32[]{:S(2)}) collective-permute-start(s32[1,1]{1,0:T(1,128)} %get-tuple-element.21), channel_id=1, source_target_pairs={{2,0},{4,2},{6,4},{3,1},{5,3},{7,5},{10,8},{12,10},{14,12},{11,9},... | collective-permute-start | bytes 20 | tf_op jit(solution)/shard_map/ppermute | solution.py:26
  16.1 4.9 %collective-permute-start.3 = (s32[1,1]{1,0:T(1,128)}, s32[1,1]{1,0:T(1,128)}, u32[]{:S(2)}, u32[]{:S(2)}) collective-permute-start(s32[1,1]{1,0:T(1,128)} %get-tuple-element.22), channel_id=1, source_target_pairs={{0,2},{2,4},{4,6},{1,3},{3,5},{5,7},{8,10},{10,12},{12,14},{9,11},... | collective-permute-start | bytes 20 | tf_op jit(solution)/shard_map/ppermute | solution.py:26
  24.0 6.7 %collective-permute-start.2 = (bf16[1,2,4,16,512]{4,3,2,1,0:T(8,128)(2,1)S(1)}, bf16[1,2,4,16,512]{4,3,2,1,0:T(8,128)(2,1)S(1)}, u32[]{:S(2)}, u32[]{:S(2)}) collective-permute-start(bf16[1,2,4,16,512]{4,3,2,1,0:T(8,128)(2,1)S(1)} %slice.64), channel_id=1, source_target_pairs={{0,2},{2,4},{4,6},{1,3},{3,5},{5,7},{8,10},{10,12},{12,14},{9,11},... | collective-permute-start | bytes 393224 | tf_op jit(solution)/shard_map/ppermute | solution.py:26
  31.0 10.2 %copy-start.2 = (bf16[1,8,2,16,512]{4,3,2,1,0:T(8,128)(2,1)S(1)}, bf16[1,8,2,16,512]{4,3,2,1,0:T(8,128)(2,1)}, u32[]{:S(2)}) copy-start(bf16[1,8,2,16,512]{4,3,2,1,0:T(8,128)(2,1)} %param.4) | copy-start | bytes 786436
  42.3 13.5 %collective-permute-start.5 = (bf16[1,4,1,16,512]{4,3,2,1,0:T(8,128)(2,1)S(1)}, bf16[1,4,1,16,512]{4,3,2,1,0:T(8,128)(2,1)S(1)}, u32[]{:S(2)}, u32[]{:S(2)}) collective-permute-start(bf16[1,4,1,16,512]{4,3,2,1,0:T(8,128)(2,1)S(1)} %get-tuple-element.16), channel_id=1, source_target_pairs={{1,0},{3,2},{5,4},{7,6},{9,8},{11,10},{13,12},{15,14},{17,16},{19,... | collective-permute-start | bytes 196616 | tf_op jit(solution)/shard_map/ppermute | solution.py:19
  45.7 10.0 %collective-permute-start.4 = (bf16[1,4,1,16,512]{4,3,2,1,0:T(8,128)(2,1)S(1)}, bf16[1,4,1,16,512]{4,3,2,1,0:T(8,128)(2,1)S(1)}, u32[]{:S(2)}, u32[]{:S(2)}) collective-permute-start(bf16[1,4,1,16,512]{4,3,2,1,0:T(8,128)(2,1)S(1)} %get-tuple-element.15), channel_id=1, source_target_pairs={{0,1},{2,3},{4,5},{6,7},{8,9},{10,11},{12,13},{14,15},{16,17},{18,... | collective-permute-start | bytes 196616 | tf_op jit(solution)/shard_map/ppermute | solution.py:18
  48.0 28.4 %all-to-all-start = ((bf16[32,16,384]{2,1,0:T(8,128)(2,1)}), bf16[32,16,384]{2,1,0:T(8,128)(2,1)S(1)}, u32[]{:S(2)}, u32[]{:S(2)}) async-start(bf16[32,16,384]{2,1,0:T(8,128)(2,1)} %bitcast.22), calls=%async_computation | async-start | bytes 786432 | tf_op jit(solution)/shard_map/all_to_all | solution.py:165
  56.8 8.1 %collective-permute-start.6 = (bf16[1,1,4,16,512]{4,3,2,1,0:T(8,128)(2,1)S(1)}, bf16[1,1,4,16,512]{4,3,2,1,0:T(8,128)(2,1)S(1)}, u32[]{:S(2)}, u32[]{:S(2)}) collective-permute-start(bf16[1,1,4,16,512]{4,3,2,1,0:T(8,128)(2,1)S(1)} %slice.68), channel_id=1, source_target_pairs={{2,0},{4,2},{6,4},{3,1},{5,3},{7,5},{10,8},{12,10},{14,12},{11,9},... | collective-permute-start | bytes 196616 | tf_op jit(solution)/shard_map/ppermute | solution.py:26
  108.0 2.2 %copy-start.1 = (bf16[4096,512]{1,0:T(8,128)(2,1)S(1)}, bf16[4096,512]{1,0:T(8,128)(2,1)}, u32[]{:S(2)}) copy-start(bf16[4096,512]{1,0:T(8,128)(2,1)} %all-gather.2.cloned.1.call-done) | copy-start | bytes 12582916
Sparse Core Ops, SparseCore 0:
  41.4 66.5 all-gather.1

commit v2 on v1

--- a/solution.py
+++ b/solution.py
@@ -64,8 +64,107 @@
         upstream[...] = (cotangent[...].astype(jnp.float32) * slope).astype(upstream.dtype)
 
 
-def backward_body(columns, height, fields, weights, out, total):
+def gather_parts(upstream, everyone, own_sem, send_sems, recv_sems):
+    here = {axis: lax.axis_index(axis) for axis in AXES}
+    size = {axis: lax.axis_size(axis) for axis in AXES}
+    dp, tm, space = (size[axis] for axis in AXES)
+    peers = {
+        axis: [lax.rem(here[axis] + k, size[axis]) for k in range(1, size[axis])] for axis in AXES
+    }
+
+    def flat(s, t, d):
+        return (s * tm + t) * dp + d
+
+    def copy(source, block, number, axis, target):
+        index = flat(*block)
+        return pltpu.make_async_remote_copy(
+            src_ref=upstream if source is None else everyone.at[index],
+            dst_ref=everyone.at[index],
+            send_sem=send_sems.at[number],
+            recv_sem=recv_sems.at[index],
+            device_id={axis: target},
+            device_id_type=pl.DeviceIdType.MESH,
+        )
+
+    mine = (here["space"], here["tm"], here["dp"])
+    column = [(here["space"], here["tm"], d) for d in peers["dp"]]
+    plane = [
+        (here["space"], t, d) for t in peers["tm"] for d in [here["dp"]] + peers["dp"]
+    ]
+    far = [
+        (s, t, d)
+        for s in peers["space"]
+        for t in [here["tm"]] + peers["tm"]
+        for d in [here["dp"]] + peers["dp"]
+    ]
+    plan, stages = [], []
+    stages.append([(None, mine, axis, p) for axis in AXES for p in peers[axis]])
+    stages.append([(1, b, axis, p) for b in column for axis in AXES[1:] for p in peers[axis]])
+    stages.append([(1, b, "space", p) for b in plane for p in peers["space"]])
+    number = 0
+    for stage in stages:
+        row = []
+        for source, block, axis, target in stage:
+            row.append(copy(source, block, number, axis, target))
+            number += 1
+        plan.append(row)
+    keep = pltpu.make_async_copy(upstream, everyone.at[flat(*mine)], own_sem)
+
+    def arrived(blocks):
+        for block in blocks:
+            copy(1, block, 0, "dp", peers["dp"][0]).wait_recv()
+
+    def begin():
+        barrier = pltpu.get_barrier_semaphore()
+        for axis in AXES:
+            for p in peers[axis]:
+                pl.semaphore_signal(
+                    barrier, inc=1, device_id={axis: p}, device_id_type=pl.DeviceIdType.MESH
+                )
+        pl.semaphore_wait(barrier, dp + tm + space - 3)
+        for one in plan[0]:
+            one.start()
+        keep.start()
+
+    def middle():
+        per_block = len(plan[1]) // len(column)
+        for k, block in enumerate(column):
+            arrived([block])
+            for one in plan[1][k * per_block : (k + 1) * per_block]:
+                one.start()
+
+    def finish():
+        per_block = len(plan[2]) // len(plane)
+        for k, block in enumerate(plane):
+            arrived([block])
+            for one in plan[2][k * per_block : (k + 1) * per_block]:
+                one.start()
+        arrived(far)
+        keep.wait()
+        for row in plan:
+            for one in row:
+                one.wait_send()
+
+    return begin, middle, finish
+
+
+def backward_body(
+    columns,
+    height,
+    fields,
+    weights,
+    upstream,
+    out,
+    everyone,
+    total,
+    own_sem,
+    send_sems,
+    recv_sems,
+):
     step = pl.program_id(0)
+    begin, middle, finish = gather_parts(upstream, everyone, own_sem, send_sems, recv_sems)
+    pl.when(step == 0)(begin)
+    pl.when(step == 4)(middle)
     place, row_tap = step // 3, step % 3
     pairs, channels = fields.shape[1], fields.shape[-1]
     source = jnp.where(place == 1, 1, 0)
@@ -103,6 +202,7 @@
     @pl.when(step == 8)
     def _():
         store(1)
+        finish()
 
 
 def weight_body(columns, rows, planes, upstream, out):
@@ -125,9 +225,9 @@
                 inside = inside & (column + right >= 0) & (column + right < columns)
                 parts.append(jnp.where(inside, moved, 0.0))
     patches = jnp.concatenate(parts, axis=0).astype(jnp.bfloat16)
-    _, tm, space, _, pairs, _, _ = upstream.shape
+    space, tm, _, _, pairs, _, _ = upstream.shape
     field = jnp.concatenate(
-        [upstream[0, t, s, 0, p] for t in range(tm) for p in range(pairs) for s in range(space)],
+        [upstream[s, t, 0, 0, p] for t in range(tm) for p in range(pairs) for s in range(space)],
         axis=0,
     )
     term = jnp.dot(patches, field, preferred_element_type=jnp.float32)
@@ -203,8 +303,7 @@
         cost_estimate=cost,
     )(taps, kernel, cotangent.reshape(cells, channels))
 
-    gathered = lax.all_gather(upstream, AXES, axis=0, tiled=True)
-
+    count = dp * tm * space
     grid = upstream.reshape(groups, pairs, height, columns, channels)
     padded = row_halo(grid)
     later = from_behind(padded[:, :1], -1)
@@ -213,23 +312,37 @@
     fields = jnp.stack([following, padded], axis=0).reshape(
         2, slots, height + 2, columns, channels
     )
-    frame_grad = pl.pallas_call(
+    frame_grad, gathered = pl.pallas_call(
         functools.partial(backward_body, columns, height),
         grid=(9,),
-        out_shape=jax.ShapeDtypeStruct((slots, 2, frame, channels), bf16),
+        out_shape=(
+            jax.ShapeDtypeStruct((slots, 2, frame, channels), bf16),
+            jax.ShapeDtypeStruct((count, cells, channels), bf16),
+        ),
         in_specs=[
             whole,
             pl.BlockSpec(
                 (1, 1, 3, channels, channels), lambda i: ((i // 3) * 2 % 3, i % 3, 0, 0, 0)
             ),
-        ],
-        out_specs=pl.BlockSpec((slots, 2, frame, channels), lambda i: (0, 0, 0, 0)),
-        scratch_shapes=[pltpu.VMEM((cells, channels), jnp.float32)],
-        compiler_params=params,
+            pl.BlockSpec(memory_space=pl.ANY),
+        ],
+        out_specs=(
+            pl.BlockSpec((slots, 2, frame, channels), lambda i: (0, 0, 0, 0)),
+            pl.BlockSpec(memory_space=pl.ANY),
+        ),
+        scratch_shapes=[
+            pltpu.VMEM((cells, channels), jnp.float32),
+            pltpu.SemaphoreType.DMA,
+            pltpu.SemaphoreType.DMA((count - 1,)),
+            pltpu.SemaphoreType.DMA((count,)),
+        ],
+        compiler_params=pltpu.CompilerParams(
+            vmem_limit_bytes=VMEM_BYTES, collective_id=0, has_side_effects=True
+        ),
         cost_estimate=cost,
-    )(fields, kernel)
-
-    per_group = gathered.reshape(dp, tm, space, groups, pairs, frame, channels)
+    )(fields, kernel, upstream)
+
+    per_group = gathered.reshape(space, tm, dp, groups, pairs, frame, channels)
     group_cells = tm * pairs * space * frame
     kernel_grad = pl.pallas_call(
         functools.partial(weight_body, columns, space * height),
@@ -238,7 +351,7 @@
         in_specs=[
             pl.BlockSpec((1, 1, 3, own, group_cells), lambda a, b: (a, b, 0, 0, 0)),
             pl.BlockSpec(
-                (1, tm, space, 1, pairs, frame, channels), lambda a, b: (a, 0, 0, b, 0, 0, 0)
+                (space, tm, 1, 1, pairs, frame, channels), lambda a, b: (0, 0, a, b, 0, 0, 0)
             ),
         ],
         out_specs=pl.BlockSpec((27 * own, channels), lambda a, b: (0, 0)),

time: 124 us -> 109 us (0.88)
  Pallas kernels: 25.4 us -> 51.4 us
  waiting for transfers between devices: 34.7 us -> 8.87 us
  between operations: 14.3 us -> 0.92 us
  starting transfers between devices: 29.8 us -> 26.4 us
  local copies, waits for them, and re-layouts: 14.3 us -> 16.9 us
    all_gather x1 -> x0, waiting for transfers between devices: 26.6 us -> none  [per_device(): gathered = lax.all_gather(upstream, AXES, axis=0, tiled=True)]
    pallas_call x1, Pallas kernels: 11.4 us -> 37.2 us  [per_device(): pl.pallas_call(functools.partial(backward_body, columns, height), grid=(9...]
    unnamed x8 -> x9, local copies, waits for them, and re-layouts: 3.18 us -> 5.81 us
    all_to_all x1, starting transfers between devices: 7.74 us -> 5.37 us  [per_device(): got = lax.all_to_all(sent, AXES, 0, 0)]
    ppermute x4, starting transfers between devices: 12.9 us -> 11.1 us  [from_behind(): lax.ppermute(value, 'tm', [(i, i + steps) for i in range(first, last)])]
  transfers between devices with their start and end apart: 10 -> 9, of which waited for: 3 -> 2; matrix products, arithmetic and copies ran while one was open for 11% -> 7% of each run, Pallas kernels for 9% -> 34%
where the time goes in v2:
time: 109 us; the launch traced here: 108 us
  Pallas kernels  51.4 us (47%)
  starting transfers between devices  26.4 us (24%)
  local copies, waits for them, and re-layouts  16.9 us (16%)
  waiting for transfers between devices  8.87 us (8%)
  other arithmetic  3.52 us (3%)
    pallas_call x1, Pallas kernels, per_device(): pl.pallas_call(functools.partial(backward_body, columns, height), grid=(9...  37.2 us
    ppermute x4, starting transfers between devices, from_behind(): lax.ppermute(value, 'tm', [(i, i + steps) for i in range(first, last)])  11.1 us
    pallas_call x1, Pallas kernels, per_device(): pl.pallas_call(functools.partial(forward_body, columns, height), grid=(9,...  10.1 us
    ppermute x4, waiting for transfers between devices, from_behind(): lax.ppermute(value, 'tm', [(i, i + steps) for i in range(first, last)])  8.85 us
    ppermute x2, starting transfers between devices, row_halo(): after = lax.ppermute(array[:, :, :1], 'space', down)  7.33 us
    unnamed x9, local copies, waits for them, and re-layouts  5.81 us
    all_to_all x1, starting transfers between devices, per_device(): got = lax.all_to_all(sent, AXES, 0, 0)  5.37 us
    pallas_call x1, Pallas kernels, per_device(): pl.pallas_call(functools.partial(weight_body, columns, space * height), g...  4.12 us
  transfers between devices with their start and end apart: 9, of which 2 were waited for; matrix products, arithmetic and copies ran while one was open for 7% of the time, Pallas kernels for 34%

profile of v2, /device:TPU:11, one launch (start us, length us, event | category | flops | bytes accessed | tf_op | source)
XLA Modules:
  0.0 108.0 jit_solution(5738725966227306904)
XLA Ops:
  0.6 1.3 %fusion.8 = (s32[1,1]{1,0:T(1,128)}, s32[1,1]{1,0:T(1,128)}) fusion(s32[1,4]{1,0:T(1,128)} %param.5), kind=kLoop, calls=%fused_computation.26 | loop fusion | bytes 16 | tf_op jit(solution)/shard_map/slice | solution.py:255
  2.0 2.2 %collective-permute-start.7 = (s32[1,1]{1,0:T(1,128)}, s32[1,1]{1,0:T(1,128)}, u32[]{:S(2)}, u32[]{:S(2)}) collective-permute-start(s32[1,1]{1,0:T(1,128)} %get-tuple-element.25), channel_id=1, source_target_pairs={{2,0},{4,2},{6,4},{3,1},{5,3},{7,5},{10,8},{12,10},{14,12},{11,9},... | collective-permute-start | bytes 20 | tf_op jit(solution)/shard_map/ppermute | solution.py:26
  4.1 4.0 %collective-permute-start.3 = (s32[1,1]{1,0:T(1,128)}, s32[1,1]{1,0:T(1,128)}, u32[]{:S(2)}, u32[]{:S(2)}) collective-permute-start(s32[1,1]{1,0:T(1,128)} %get-tuple-element.26), channel_id=1, source_target_pairs={{0,2},{2,4},{4,6},{1,3},{3,5},{5,7},{8,10},{10,12},{12,14},{9,11},... | collective-permute-start | bytes 20 | tf_op jit(solution)/shard_map/ppermute | solution.py:26
  8.1 1.0 fusion.5
  9.1 3.1 %collective-permute-start.1 = (bf16[1,8,1,16,512]{4,3,2,1,0:T(8,128)(2,1)S(1)}, bf16[1,8,1,16,512]{4,3,2,1,0:T(8,128)(2,1)S(1)}, u32[]{:S(2)}, u32[]{:S(2)}) collective-permute-start(bf16[1,8,1,16,512]{4,3,2,1,0:T(8,128)(2,1)S(1)} %get-tuple-element.17), channel_id=1, source_target_pairs={{1,0},{3,2},{5,4},{7,6},{9,8},{11,10},{13,12},{15,14},{17,16},{19,... | collective-permute-start | bytes 393224 | tf_op jit(solution)/shard_map/ppermute | solution.py:19
  12.3 1.3 %collective-permute-start = (bf16[1,8,1,16,512]{4,3,2,1,0:T(8,128)(2,1)S(1)}, bf16[1,8,1,16,512]{4,3,2,1,0:T(8,128)(2,1)S(1)}, u32[]{:S(2)}, u32[]{:S(2)}) collective-permute-start(bf16[1,8,1,16,512]{4,3,2,1,0:T(8,128)(2,1)S(1)} %get-tuple-element.18), channel_id=1, source_target_pairs={{0,1},{2,3},{4,5},{6,7},{8,9},{10,11},{12,13},{14,15},{16,17},{18,... | collective-permute-start | bytes 393224 | tf_op jit(solution)/shard_map/ppermute | solution.py:18
  15.3 2.0 %fusion.3 = (bf16[4]{0:T(256)(128)(2,1)S(1)}, bf16[4]{0:T(256)(128)(2,1)S(1)}) fusion(s32[1,4]{1,0:T(1,128)} %param.5, s32[1,1]{1,0:T(1,128)} %collective-permute-done.7, s32[1,3]{1,0:T(1,128)S(1)} %get-tuple-element.23, s32[1,3]{1,0:T(1,128)S(1)} %get-tuple-element.24, s32[1,1]{1,0:T(1,128)} %collective-permute-done.3), kind=kLoop, calls=%fused_computation.21 | loop fusion | flops 24 | bytes 64 | tf_op jit(solution)/shard_map/mul | solution.py:311
  17.3 1.1 broadcast_multiply_fusion
  18.4 1.0 constant_dynamic-update-slice_fusion.1
  19.4 2.7 %collective-permute-start.2 = (bf16[1,2,4,16,512]{4,3,2,1,0:T(8,128)(2,1)S(1)}, bf16[1,2,4,16,512]{4,3,2,1,0:T(8,128)(2,1)S(1)}, u32[]{:S(2)}, u32[]{:S(2)}) collective-permute-start(bf16[1,2,4,16,512]{4,3,2,1,0:T(8,128)(2,1)S(1)} %slice.64), channel_id=1, source_target_pairs={{0,2},{2,4},{4,6},{1,3},{3,5},{5,7},{8,10},{10,12},{12,14},{9,11},... | collective-permute-start | bytes 393224 | tf_op jit(solution)/shard_map/ppermute | solution.py:26
  22.2 2.9 %collective-permute-done.2 = bf16[1,2,4,16,512]{4,3,2,1,0:T(8,128)(2,1)S(1)} collective-permute-done((bf16[1,2,4,16,512]{4,3,2,1,0:T(8,128)(2,1)S(1)}, bf16[1,2,4,16,512]{4,3,2,1,0:T(8,128)(2,1)S(1)}, u32[]{:S(2)}, u32[]{:S(2)}) %collective-permute-start.2) | collective-permute-done | bytes 131104 | tf_op jit(solution)/shard_map/ppermute | solution.py:26
  25.4 10.1 %shard_map.67 = (bf16[128,512]{1,0:T(8,128)(2,1)}, bf16[128,512]{1,0:T(8,128)(2,1)S(1)}) custom-call(bf16[3,4,4,16,512]{4,3,2,1,0:T(8,128)(2,1)S(1)} %maximum_bitcast_fusion.planes, bf16[3,3,3,512,512]{4,3,2,1,0:T(8,128)(2,1)} %weights.3, bf16[128,512]{1,0:T(8,128)(2,1)S(1)} %bitcast.51), custom_call_target="tpu_custom_call" | custom-call | flops 1811939328 | bytes 14155776 | tf_op jit(solution)/shard_map/pallas_call | solution.py:288
  35.6 1.3 %collective-permute-start.4 = (bf16[1,4,1,16,512]{4,3,2,1,0:T(8,128)(2,1)S(1)}, bf16[1,4,1,16,512]{4,3,2,1,0:T(8,128)(2,1)S(1)}, u32[]{:S(2)}, u32[]{:S(2)}) collective-permute-start(bf16[1,4,1,16,512]{4,3,2,1,0:T(8,128)(2,1)S(1)} %get-tuple-element.19), channel_id=1, source_target_pairs={{0,1},{2,3},{4,5},{6,7},{8,9},{10,11},{12,13},{14,15},{16,17},{18,... | collective-permute-start | bytes 196616 | tf_op jit(solution)/shard_map/ppermute | solution.py:18
  36.9 4.2 %collective-permute-start.5 = (bf16[1,4,1,16,512]{4,3,2,1,0:T(8,128)(2,1)S(1)}, bf16[1,4,1,16,512]{4,3,2,1,0:T(8,128)(2,1)S(1)}, u32[]{:S(2)}, u32[]{:S(2)}) collective-permute-start(bf16[1,4,1,16,512]{4,3,2,1,0:T(8,128)(2,1)S(1)} %get-tuple-element.20), channel_id=1, source_target_pairs={{1,0},{3,2},{5,4},{7,6},{9,8},{11,10},{13,12},{15,14},{17,16},{19,... | collective-permute-start | bytes 196616 | tf_op jit(solution)/shard_map/ppermute | solution.py:19
  42.0 5.4 %all-to-all-start = ((bf16[32,16,384]{2,1,0:T(8,128)(2,1)}), bf16[32,16,384]{2,1,0:T(8,128)(2,1)S(1)}, u32[]{:S(2)}, u32[]{:S(2)}) async-start(bf16[32,16,384]{2,1,0:T(8,128)(2,1)} %bitcast.22), calls=%async_computation | async-start | bytes 786432 | tf_op jit(solution)/shard_map/all_to_all | solution.py:265
  47.5 2.2 %collective-permute-start.6 = (bf16[1,1,4,16,512]{4,3,2,1,0:T(8,128)(2,1)S(1)}, bf16[1,1,4,16,512]{4,3,2,1,0:T(8,128)(2,1)S(1)}, u32[]{:S(2)}, u32[]{:S(2)}) collective-permute-start(bf16[1,1,4,16,512]{4,3,2,1,0:T(8,128)(2,1)S(1)} %slice.68), channel_id=1, source_target_pairs={{2,0},{4,2},{6,4},{3,1},{5,3},{7,5},{10,8},{12,10},{14,12},{11,9},... | collective-permute-start | bytes 196616 | tf_op jit(solution)/shard_map/ppermute | solution.py:26
  49.7 5.9 %collective-permute-done.6 = bf16[1,1,4,16,512]{4,3,2,1,0:T(8,128)(2,1)S(1)} collective-permute-done((bf16[1,1,4,16,512]{4,3,2,1,0:T(8,128)(2,1)S(1)}, bf16[1,1,4,16,512]{4,3,2,1,0:T(8,128)(2,1)S(1)}, u32[]{:S(2)}, u32[]{:S(2)}) %collective-permute-start.6) | collective-permute-done | bytes 65568 | tf_op jit(solution)/shard_map/ppermute | solution.py:26
  55.8 37.2 %shard_map.68 = (bf16[4,2,32,512]{3,2,1,0:T(8,128)(2,1)S(1)}, bf16[32,128,512]{2,1,0:T(8,128)(2,1)S(1)}) custom-call(bf16[2,4,4,16,512]{4,3,2,1,0:T(8,128)(2,1)S(1)} %maximum_bitcast_fusion.1.fields, bf16[3,3,3,512,512]{4,3,2,1,0:T(8,128)(2,1)} %weights.3, bf16[128,512]{1,0:T(8,128)(2,1)S(1)} %get-tuple-element.8.upstream), custom_call_target="tpu_custom_call" | custom-call | flops 1811939328 | bytes 14155776 | tf_op jit(solution)/shard_map/pallas_call | solution.py:315
  93.0 1.9 %copy-done.1 = bf16[32,128,512]{2,1,0:T(8,128)(2,1)} copy-done((bf16[32,128,512]{2,1,0:T(8,128)(2,1)}, bf16[32,128,512]{2,1,0:T(8,128)(2,1)S(1)}, u32[]{:S(2)}) %copy-start.1) | copy-done | bytes 4194328
  95.8 2.4 %copy.27 = bf16[4,1,3,16,4,4,2,32]{7,6,5,4,3,2,0,1:T(2,128)(2,1)S(1)} copy(bf16[4,1,3,16,4,4,2,32]{7,5,2,3,6,4,0,1:T(4,128)(2,1)S(1)} %bitcast.53) | data formatting | bytes 786432 | tf_op jit(solution)/shard_map/transpose | solution.py:267
  98.2 1.6 %reshape.123.planes = bf16[4,1,3,16,1024]{4,3,2,1,0:T(8,128)(2,1)S(1)} reshape(bf16[4,1,3,16,4,4,2,32]{7,6,5,4,3,2,0,1:T(2,128)(2,1)S(1)} %copy.27) | data formatting | bytes 786432 | tf_op jit(solution)/shard_map/reshape | solution.py:267
  99.9 2.2 %copy-done.2 = bf16[32,128,512]{2,1,0:T(8,128)(2,1)S(1)} copy-done((bf16[32,128,512]{2,1,0:T(8,128)(2,1)S(1)}, bf16[32,128,512]{2,1,0:T(8,128)(2,1)}, u32[]{:S(2)}) %copy-start.2) | copy-done | bytes 4194328
  102.0 4.1 %shard_map.69 = f32[432,512]{1,0:T(8,128)S(1)} custom-call(bf16[4,1,3,16,1024]{4,3,2,1,0:T(8,128)(2,1)S(1)} %reshape.123.planes, bf16[2,4,4,1,4,32,512]{6,5,4,3,2,1,0:T(8,128)(2,1)S(1)} %bitcast.52), custom_call_target="tpu_custom_call" | custom-call | flops 1811939328 | bytes 4194304 | tf_op jit(solution)/shard_map/pallas_call | solution.py:347
  106.2 1.2 %reshape.125 = f32[27,8192]{1,0:T(8,128)} reshape(f32[432,512]{1,0:T(8,128)S(1)} %shard_map.69) | data formatting | bytes 1769472 | tf_op jit(solution)/shard_map/reshape | solution.py:367
  (30 shorter events, 4.8 us)
Async XLA Ops:
  0.6 24.8 %copy-start = (bf16[1,4,2,16,512]{4,3,2,1,0:T(8,128)(2,1)S(1)}, bf16[1,4,2,16,512]{4,3,2,1,0:T(8,128)(2,1)}, u32[]{:S(2)}) copy-start(bf16[1,4,2,16,512]{4,3,2,1,0:T(8,128)(2,1)} %param.7) | copy-start | bytes 393220
  2.0 13.4 %collective-permute-start.7 = (s32[1,1]{1,0:T(1,128)}, s32[1,1]{1,0:T(1,128)}, u32[]{:S(2)}, u32[]{:S(2)}) collective-permute-start(s32[1,1]{1,0:T(1,128)} %get-tuple-element.25), channel_id=1, source_target_pairs={{2,0},{4,2},{6,4},{3,1},{5,3},{7,5},{10,8},{12,10},{14,12},{11,9},... | collective-permute-start | bytes 20 | tf_op jit(solution)/shard_map/ppermute | solution.py:26
  4.1 11.2 %collective-permute-start.3 = (s32[1,1]{1,0:T(1,128)}, s32[1,1]{1,0:T(1,128)}, u32[]{:S(2)}, u32[]{:S(2)}) collective-permute-start(s32[1,1]{1,0:T(1,128)} %get-tuple-element.26), channel_id=1, source_target_pairs={{0,2},{2,4},{4,6},{1,3},{3,5},{5,7},{8,10},{10,12},{12,14},{9,11},... | collective-permute-start | bytes 20 | tf_op jit(solution)/shard_map/ppermute | solution.py:26
  9.1 10.2 %collective-permute-start.1 = (bf16[1,8,1,16,512]{4,3,2,1,0:T(8,128)(2,1)S(1)}, bf16[1,8,1,16,512]{4,3,2,1,0:T(8,128)(2,1)S(1)}, u32[]{:S(2)}, u32[]{:S(2)}) collective-permute-start(bf16[1,8,1,16,512]{4,3,2,1,0:T(8,128)(2,1)S(1)} %get-tuple-element.17), channel_id=1, source_target_pairs={{1,0},{3,2},{5,4},{7,6},{9,8},{11,10},{13,12},{15,14},{17,16},{19,... | collective-permute-start | bytes 393224 | tf_op jit(solution)/shard_map/ppermute | solution.py:19
  12.3 6.1 %collective-permute-start = (bf16[1,8,1,16,512]{4,3,2,1,0:T(8,128)(2,1)S(1)}, bf16[1,8,1,16,512]{4,3,2,1,0:T(8,128)(2,1)S(1)}, u32[]{:S(2)}, u32[]{:S(2)}) collective-permute-start(bf16[1,8,1,16,512]{4,3,2,1,0:T(8,128)(2,1)S(1)} %get-tuple-element.18), channel_id=1, source_target_pairs={{0,1},{2,3},{4,5},{6,7},{8,9},{10,11},{12,13},{14,15},{16,17},{18,... | collective-permute-start | bytes 393224 | tf_op jit(solution)/shard_map/ppermute | solution.py:18
  19.4 5.7 %collective-permute-start.2 = (bf16[1,2,4,16,512]{4,3,2,1,0:T(8,128)(2,1)S(1)}, bf16[1,2,4,16,512]{4,3,2,1,0:T(8,128)(2,1)S(1)}, u32[]{:S(2)}, u32[]{:S(2)}) collective-permute-start(bf16[1,2,4,16,512]{4,3,2,1,0:T(8,128)(2,1)S(1)} %slice.64), channel_id=1, source_target_pairs={{0,2},{2,4},{4,6},{1,3},{3,5},{5,7},{8,10},{10,12},{12,14},{9,11},... | collective-permute-start | bytes 393224 | tf_op jit(solution)/shard_map/ppermute | solution.py:26
  35.6 11.8 %collective-permute-start.4 = (bf16[1,4,1,16,512]{4,3,2,1,0:T(8,128)(2,1)S(1)}, bf16[1,4,1,16,512]{4,3,2,1,0:T(8,128)(2,1)S(1)}, u32[]{:S(2)}, u32[]{:S(2)}) collective-permute-start(bf16[1,4,1,16,512]{4,3,2,1,0:T(8,128)(2,1)S(1)} %get-tuple-element.19), channel_id=1, source_target_pairs={{0,1},{2,3},{4,5},{6,7},{8,9},{10,11},{12,13},{14,15},{16,17},{18,... | collective-permute-start | bytes 196616 | tf_op jit(solution)/shard_map/ppermute | solution.py:18
  36.9 10.6 %collective-permute-start.5 = (bf16[1,4,1,16,512]{4,3,2,1,0:T(8,128)(2,1)S(1)}, bf16[1,4,1,16,512]{4,3,2,1,0:T(8,128)(2,1)S(1)}, u32[]{:S(2)}, u32[]{:S(2)}) collective-permute-start(bf16[1,4,1,16,512]{4,3,2,1,0:T(8,128)(2,1)S(1)} %get-tuple-element.20), channel_id=1, source_target_pairs={{1,0},{3,2},{5,4},{7,6},{9,8},{11,10},{13,12},{15,14},{17,16},{19,... | collective-permute-start | bytes 196616 | tf_op jit(solution)/shard_map/ppermute | solution.py:19
  42.0 52.9 %all-to-all-start = ((bf16[32,16,384]{2,1,0:T(8,128)(2,1)}), bf16[32,16,384]{2,1,0:T(8,128)(2,1)S(1)}, u32[]{:S(2)}, u32[]{:S(2)}) async-start(bf16[32,16,384]{2,1,0:T(8,128)(2,1)} %bitcast.22), calls=%async_computation | async-start | bytes 786432 | tf_op jit(solution)/shard_map/all_to_all | solution.py:265
  47.5 8.1 %collective-permute-start.6 = (bf16[1,1,4,16,512]{4,3,2,1,0:T(8,128)(2,1)S(1)}, bf16[1,1,4,16,512]{4,3,2,1,0:T(8,128)(2,1)S(1)}, u32[]{:S(2)}, u32[]{:S(2)}) collective-permute-start(bf16[1,1,4,16,512]{4,3,2,1,0:T(8,128)(2,1)S(1)} %slice.68), channel_id=1, source_target_pairs={{2,0},{4,2},{6,4},{3,1},{5,3},{7,5},{10,8},{12,10},{14,12},{11,9},... | collective-permute-start | bytes 196616 | tf_op jit(solution)/shard_map/ppermute | solution.py:26
  92.9 1.9 %copy-start.1 = (bf16[32,128,512]{2,1,0:T(8,128)(2,1)}, bf16[32,128,512]{2,1,0:T(8,128)(2,1)S(1)}, u32[]{:S(2)}) copy-start(bf16[32,128,512]{2,1,0:T(8,128)(2,1)S(1)} %get-tuple-element.10) | copy-start | bytes 12582916
  99.8 2.2 %copy-start.2 = (bf16[32,128,512]{2,1,0:T(8,128)(2,1)S(1)}, bf16[32,128,512]{2,1,0:T(8,128)(2,1)}, u32[]{:S(2)}) copy-start(bf16[32,128,512]{2,1,0:T(8,128)(2,1)} %copy-done.1) | copy-start | bytes 12582916

commit v3 on v2

--- a/solution.py
+++ b/solution.py
@@ -24,6 +24,23 @@
     count = lax.axis_size("tm")
     first, last = max(0, -steps), min(count, count - steps)
     return lax.ppermute(value, "tm", [(i, i + steps) for i in range(first, last)])
+
+
+def haloed_from_behind(value, steps):
+    count, size = lax.axis_size("tm"), lax.axis_size("space")
+
+    def edge(rows, move):
+        perm = [
+            (t * size + s, (t + steps) * size + s + move)
+            for t in range(max(0, -steps), min(count, count - steps))
+            for s in range(max(0, -move), min(size, size - move))
+        ]
+        return lax.ppermute(rows, ("tm", "space"), perm)
+
+    middle = from_behind(value, steps)
+    before = edge(value[:, :, -1:], 1)
+    after = edge(value[:, :, :1], -1)
+    return jnp.concatenate([before, middle, after], axis=2)
 
 
 def column_taps(base, columns):
@@ -267,7 +284,7 @@
     own_planes = got.transpose(0, 5, 4, 3, 1, 6, 2, 7).reshape(dp, groups, 3, own, -1)
 
     rowed = row_halo(frames)
-    earlier = from_behind(rowed[:, -2:], 1)
+    earlier = haloed_from_behind(frames[:, -2:], 1)
     extended = jnp.concatenate([earlier, rowed], axis=1)
     gate = linked[:, :, None, None, None]
     taps = jnp.stack(
@@ -306,7 +323,7 @@
     count = dp * tm * space
     grid = upstream.reshape(groups, pairs, height, columns, channels)
     padded = row_halo(grid)
-    later = from_behind(padded[:, :1], -1)
+    later = haloed_from_behind(grid[:, :1], -1)
     following = jnp.concatenate([padded[:, 1:], later], axis=1)
     following = following * onward[:, :, None, None, None]
     fields = jnp.stack([following, padded], axis=0).reshape(

time: 109 us -> 116 us (1.064)
  waiting for transfers between devices: 8.87 us -> 1.12 us
  local copies, waits for them, and re-layouts: 16.9 us -> 22 us
  starting transfers between devices: 26.4 us -> 31.4 us
  Pallas kernels: 51.4 us -> 54.9 us
    ppermute x0 -> x4, starting transfers between devices: none -> 8.21 us  [edge(): return lax.ppermute(rows, ('tm', 'space'), perm)]
    ppermute x4, waiting for transfers between devices: 8.85 us -> 1.09 us  [from_behind(): lax.ppermute(value, 'tm', [(i, i + steps) for i in range(first, last)])]
    pallas_call x1, Pallas kernels: 37.2 us -> 40.7 us  [per_device(): pl.pallas_call(functools.partial(backward_body, columns, height), grid=(9...]
    reshape x1, local copies, waits for them, and re-layouts: 1.6 us -> 4.86 us  [per_device(): got.transpose(0, 5, 4, 3, 1, 6, 2, 7).reshape(dp, groups, 3, own, -1)]
    ppermute x2, starting transfers between devices: 7.33 us -> 4.71 us  [row_halo(): after = lax.ppermute(array[:, :, :1], 'space', down)]
    slice x2 -> x4, local copies, waits for them, and re-layouts: 0.02 us -> 1.64 us  [the longest x1 0.85 us: per_device(): earlier = haloed_from_behind(frames[:, -2:], 1)]
    transpose x1, local copies, waits for them, and re-layouts: 2.43 us -> 3.6 us  [per_device(): got.transpose(0, 5, 4, 3, 1, 6, 2, 7).reshape(dp, groups, 3, own, -1)]
    unnamed x9 -> x11, local copies, waits for them, and re-layouts: 5.81 us -> 4.87 us
  transfers between devices with their start and end apart: 9 -> 13, of which waited for: 2 -> 1; matrix products, arithmetic and copies ran while one was open for 7% -> 8% of each run, Pallas kernels for 34% -> 45%
where the time goes in v3:
time: 116 us; the launch traced here: 114 us
  Pallas kernels  54.9 us (47%)
  starting transfers between devices  31.4 us (27%)
  local copies, waits for them, and re-layouts  22 us (19%)
  other arithmetic  3.57 us (3%)
    pallas_call x1, Pallas kernels, per_device(): pl.pallas_call(functools.partial(backward_body, columns, height), grid=(9...  40.7 us
    pallas_call x1, Pallas kernels, per_device(): pl.pallas_call(functools.partial(forward_body, columns, height), grid=(9,...  10.1 us
    ppermute x4, starting transfers between devices, from_behind(): lax.ppermute(value, 'tm', [(i, i + steps) for i in range(first, last)])  10 us
    ppermute x4, starting transfers between devices, edge(): return lax.ppermute(rows, ('tm', 'space'), perm)  8.21 us
    all_to_all x1, starting transfers between devices, per_device(): got = lax.all_to_all(sent, AXES, 0, 0)  5.89 us
    unnamed x11, local copies, waits for them, and re-layouts  4.87 us
    reshape x1, local copies, waits for them, and re-layouts, per_device(): got.transpose(0, 5, 4, 3, 1, 6, 2, 7).reshape(dp, groups, 3, own, -1)  4.86 us
    ppermute x2, starting transfers between devices, row_halo(): after = lax.ppermute(array[:, :, :1], 'space', down)  4.71 us
  transfers between devices with their start and end apart: 13, of which 1 were waited for; matrix products, arithmetic and copies ran while one was open for 8% of the time, Pallas kernels for 45%

profile of v3, /device:TPU:11, one launch (start us, length us, event | category | flops | bytes accessed | tf_op | source)
XLA Modules:
  0.0 114.0 jit_solution(11201070090836098911)
XLA Ops:
  0.6 1.3 %fusion.10 = (s32[1,1]{1,0:T(1,128)}, s32[1,1]{1,0:T(1,128)}) fusion(s32[1,4]{1,0:T(1,128)} %param.5), kind=kLoop, calls=%fused_computation.29 | loop fusion | bytes 16 | tf_op jit(solution)/shard_map/slice | solution.py:272
  2.0 2.2 %collective-permute-start.11 = (s32[1,1]{1,0:T(1,128)}, s32[1,1]{1,0:T(1,128)}, u32[]{:S(2)}, u32[]{:S(2)}) collective-permute-start(s32[1,1]{1,0:T(1,128)} %get-tuple-element.29), channel_id=1, source_target_pairs={{2,0},{4,2},{6,4},{3,1},{5,3},{7,5},{10,8},{12,10},{14,12},{11,9},... | collective-permute-start | bytes 20 | tf_op jit(solution)/shard_map/ppermute | solution.py:26
  4.1 4.0 %collective-permute-start.5 = (s32[1,1]{1,0:T(1,128)}, s32[1,1]{1,0:T(1,128)}, u32[]{:S(2)}, u32[]{:S(2)}) collective-permute-start(s32[1,1]{1,0:T(1,128)} %get-tuple-element.30), channel_id=1, source_target_pairs={{0,2},{2,4},{4,6},{1,3},{3,5},{5,7},{8,10},{10,12},{12,14},{9,11},... | collective-permute-start | bytes 20 | tf_op jit(solution)/shard_map/ppermute | solution.py:26
  8.9 1.3 %collective-permute-start = (bf16[1,2,1,16,512]{4,3,2,1,0:T(8,128)(2,1)S(1)}, bf16[1,2,1,16,512]{4,3,2,1,0:T(8,128)(2,1)S(1)}, u32[]{:S(2)}, u32[]{:S(2)}) collective-permute-start(bf16[1,2,1,16,512]{4,3,2,1,0:T(8,128)(2,1)S(1)} %get-tuple-element.17), channel_id=1, source_target_pairs={{0,3},{2,5},{4,7},{8,11},{10,13},{12,15},{16,19},{18,21},{20,23},{... | collective-permute-start | bytes 98312 | tf_op jit(solution)/shard_map/ppermute | solution.py:38
  10.2 3.8 %collective-permute-start.2 = (bf16[1,2,1,16,512]{4,3,2,1,0:T(8,128)(2,1)S(1)}, bf16[1,2,1,16,512]{4,3,2,1,0:T(8,128)(2,1)S(1)}, u32[]{:S(2)}, u32[]{:S(2)}) collective-permute-start(bf16[1,2,1,16,512]{4,3,2,1,0:T(8,128)(2,1)S(1)} %get-tuple-element.18), channel_id=1, source_target_pairs={{1,2},{3,4},{5,6},{9,10},{11,12},{13,14},{17,18},{19,20},{21,22},{... | collective-permute-start | bytes 98312 | tf_op jit(solution)/shard_map/ppermute | solution.py:38
  14.9 1.9 %collective-permute-start.1 = (bf16[1,2,2,16,512]{4,3,2,1,0:T(8,128)(2,1)S(1)}, bf16[1,2,2,16,512]{4,3,2,1,0:T(8,128)(2,1)S(1)}, u32[]{:S(2)}, u32[]{:S(2)}) collective-permute-start(bf16[1,2,2,16,512]{4,3,2,1,0:T(8,128)(2,1)S(1)} %slice.65), channel_id=1, source_target_pairs={{0,2},{2,4},{4,6},{1,3},{3,5},{5,7},{8,10},{10,12},{12,14},{9,11},... | collective-permute-start | bytes 196616 | tf_op jit(solution)/shard_map/ppermute | solution.py:26
  19.6 1.7 %collective-permute-start.4 = (bf16[1,8,1,16,512]{4,3,2,1,0:T(8,128)(2,1)S(1)}, bf16[1,8,1,16,512]{4,3,2,1,0:T(8,128)(2,1)S(1)}, u32[]{:S(2)}, u32[]{:S(2)}) collective-permute-start(bf16[1,8,1,16,512]{4,3,2,1,0:T(8,128)(2,1)S(1)} %get-tuple-element.19), channel_id=1, source_target_pairs={{1,0},{3,2},{5,4},{7,6},{9,8},{11,10},{13,12},{15,14},{17,16},{19,... | collective-permute-start | bytes 393224 | tf_op jit(solution)/shard_map/ppermute | solution.py:19
  21.3 1.3 %collective-permute-start.3 = (bf16[1,8,1,16,512]{4,3,2,1,0:T(8,128)(2,1)S(1)}, bf16[1,8,1,16,512]{4,3,2,1,0:T(8,128)(2,1)S(1)}, u32[]{:S(2)}, u32[]{:S(2)}) collective-permute-start(bf16[1,8,1,16,512]{4,3,2,1,0:T(8,128)(2,1)S(1)} %get-tuple-element.20), channel_id=1, source_target_pairs={{0,1},{2,3},{4,5},{6,7},{8,9},{10,11},{12,13},{14,15},{16,17},{18,... | collective-permute-start | bytes 393224 | tf_op jit(solution)/shard_map/ppermute | solution.py:18
  22.6 2.0 %fusion.3 = (bf16[4]{0:T(256)(128)(2,1)S(1)}, bf16[4]{0:T(256)(128)(2,1)S(1)}) fusion(s32[1,4]{1,0:T(1,128)} %param.5, s32[1,1]{1,0:T(1,128)} %collective-permute-done.11, s32[1,3]{1,0:T(1,128)S(1)} %get-tuple-element.27, s32[1,3]{1,0:T(1,128)S(1)} %get-tuple-element.28, s32[1,1]{1,0:T(1,128)} %collective-permute-done.5), kind=kLoop, calls=%fused_computation.22 | loop fusion | flops 24 | bytes 64 | tf_op jit(solution)/shard_map/mul | solution.py:328
  24.5 1.1 broadcast_multiply_fusion
  26.6 5.9 %all-to-all-start = ((bf16[32,16,384]{2,1,0:T(8,128)(2,1)}), bf16[32,16,384]{2,1,0:T(8,128)(2,1)S(1)}, u32[]{:S(2)}, u32[]{:S(2)}) async-start(bf16[32,16,384]{2,1,0:T(8,128)(2,1)} %bitcast.22), calls=%async_computation | async-start | bytes 786432 | tf_op jit(solution)/shard_map/all_to_all | solution.py:282
  32.9 10.1 %shard_map.67 = (bf16[128,512]{1,0:T(8,128)(2,1)}, bf16[128,512]{1,0:T(8,128)(2,1)S(1)}) custom-call(bf16[3,4,4,16,512]{4,3,2,1,0:T(8,128)(2,1)S(1)} %maximum_bitcast_fusion.planes, bf16[3,3,3,512,512]{4,3,2,1,0:T(8,128)(2,1)} %weights.3, bf16[128,512]{1,0:T(8,128)(2,1)S(1)} %bitcast.54), custom_call_target="tpu_custom_call" | custom-call | flops 1811939328 | bytes 14155776 | tf_op jit(solution)/shard_map/pallas_call | solution.py:305
  43.1 1.3 %collective-permute-start.8 = (bf16[1,1,1,16,512]{4,3,2,1,0:T(8,128)(2,1)S(1)}, bf16[1,1,1,16,512]{4,3,2,1,0:T(8,128)(2,1)S(1)}, u32[]{:S(2)}, u32[]{:S(2)}) collective-permute-start(bf16[1,1,1,16,512]{4,3,2,1,0:T(8,128)(2,1)S(1)} %get-tuple-element.21), channel_id=1, source_target_pairs={{2,1},{4,3},{6,5},{10,9},{12,11},{14,13},{18,17},{20,19},{22,21},{... | collective-permute-start | bytes 49160 | tf_op jit(solution)/shard_map/ppermute | solution.py:38
  44.4 1.8 %collective-permute-start.10 = (bf16[1,1,1,16,512]{4,3,2,1,0:T(8,128)(2,1)S(1)}, bf16[1,1,1,16,512]{4,3,2,1,0:T(8,128)(2,1)S(1)}, u32[]{:S(2)}, u32[]{:S(2)}) collective-permute-start(bf16[1,1,1,16,512]{4,3,2,1,0:T(8,128)(2,1)S(1)} %get-tuple-element.22), channel_id=1, source_target_pairs={{3,0},{5,2},{7,4},{11,8},{13,10},{15,12},{19,16},{21,18},{23,20},{... | collective-permute-start | bytes 49160 | tf_op jit(solution)/shard_map/ppermute | solution.py:38
  46.2 1.9 %collective-permute-start.9 = (bf16[1,1,2,16,512]{4,3,2,1,0:T(8,128)(2,1)S(1)}, bf16[1,1,2,16,512]{4,3,2,1,0:T(8,128)(2,1)S(1)}, u32[]{:S(2)}, u32[]{:S(2)}) collective-permute-start(bf16[1,1,2,16,512]{4,3,2,1,0:T(8,128)(2,1)S(1)} %slice.88), channel_id=1, source_target_pairs={{2,0},{4,2},{6,4},{3,1},{5,3},{7,5},{10,8},{12,10},{14,12},{11,9},... | collective-permute-start | bytes 98312 | tf_op jit(solution)/shard_map/ppermute | solution.py:26
  48.1 1.3 %collective-permute-start.6 = (bf16[1,4,1,16,512]{4,3,2,1,0:T(8,128)(2,1)S(1)}, bf16[1,4,1,16,512]{4,3,2,1,0:T(8,128)(2,1)S(1)}, u32[]{:S(2)}, u32[]{:S(2)}) collective-permute-start(bf16[1,4,1,16,512]{4,3,2,1,0:T(8,128)(2,1)S(1)} %get-tuple-element.23), channel_id=1, source_target_pairs={{0,1},{2,3},{4,5},{6,7},{8,9},{10,11},{12,13},{14,15},{16,17},{18,... | collective-permute-start | bytes 196616 | tf_op jit(solution)/shard_map/ppermute | solution.py:18
  49.4 3.0 %collective-permute-start.7 = (bf16[1,4,1,16,512]{4,3,2,1,0:T(8,128)(2,1)S(1)}, bf16[1,4,1,16,512]{4,3,2,1,0:T(8,128)(2,1)S(1)}, u32[]{:S(2)}, u32[]{:S(2)}) collective-permute-start(bf16[1,4,1,16,512]{4,3,2,1,0:T(8,128)(2,1)S(1)} %get-tuple-element.24), channel_id=1, source_target_pairs={{1,0},{3,2},{5,4},{7,6},{9,8},{11,10},{13,12},{15,14},{17,16},{19,... | collective-permute-start | bytes 196616 | tf_op jit(solution)/shard_map/ppermute | solution.py:19
  53.8 40.7 %shard_map.68 = (bf16[4,2,32,512]{3,2,1,0:T(8,128)(2,1)S(1)}, bf16[32,128,512]{2,1,0:T(8,128)(2,1)S(1)}) custom-call(bf16[2,4,4,16,512]{4,3,2,1,0:T(8,128)(2,1)S(1)} %maximum_bitcast_fusion.1.fields, bf16[3,3,3,512,512]{4,3,2,1,0:T(8,128)(2,1)} %weights.3, bf16[128,512]{1,0:T(8,128)(2,1)S(1)} %get-tuple-element.8.upstream), custom_call_target="tpu_custom_call" | custom-call | flops 1811939328 | bytes 14155776 | tf_op jit(solution)/shard_map/pallas_call | solution.py:332
  94.6 1.9 %copy-done.1 = bf16[32,128,512]{2,1,0:T(8,128)(2,1)} copy-done((bf16[32,128,512]{2,1,0:T(8,128)(2,1)}, bf16[32,128,512]{2,1,0:T(8,128)(2,1)S(1)}, u32[]{:S(2)}) %copy-start.1) | copy-done | bytes 4194328
  97.4 3.6 %copy.27 = bf16[4,1,3,16,4,4,2,32]{7,6,5,4,3,2,0,1:T(2,128)(2,1)} copy(bf16[4,1,3,16,4,4,2,32]{7,5,2,3,6,4,0,1:T(4,128)(2,1)S(1)} %bitcast.56) | data formatting | bytes 786432 | tf_op jit(solution)/shard_map/transpose | solution.py:284
  101.0 4.9 %reshape.123.planes = bf16[4,1,3,16,1024]{4,3,2,1,0:T(8,128)(2,1)S(1)} reshape(bf16[4,1,3,16,4,4,2,32]{7,6,5,4,3,2,0,1:T(2,128)(2,1)} %copy.27) | data formatting | bytes 786432 | tf_op jit(solution)/shard_map/reshape | solution.py:284
  105.9 2.2 %copy-done.2 = bf16[32,128,512]{2,1,0:T(8,128)(2,1)S(1)} copy-done((bf16[32,128,512]{2,1,0:T(8,128)(2,1)S(1)}, bf16[32,128,512]{2,1,0:T(8,128)(2,1)}, u32[]{:S(2)}) %copy-start.2) | copy-done | bytes 4194328
  108.1 4.1 %shard_map.69 = f32[432,512]{1,0:T(8,128)S(1)} custom-call(bf16[4,1,3,16,1024]{4,3,2,1,0:T(8,128)(2,1)S(1)} %reshape.123.planes, bf16[2,4,4,1,4,32,512]{6,5,4,3,2,1,0:T(8,128)(2,1)S(1)} %bitcast.55), custom_call_target="tpu_custom_call" | custom-call | flops 1811939328 | bytes 4194304 | tf_op jit(solution)/shard_map/pallas_call | solution.py:364
  112.2 1.2 %reshape.125 = f32[27,8192]{1,0:T(8,128)} reshape(f32[432,512]{1,0:T(8,128)S(1)} %shard_map.69) | data formatting | bytes 1769472 | tf_op jit(solution)/shard_map/reshape | solution.py:384
  (42 shorter events, 8.6 us)
Async XLA Ops:
  0.6 31.9 %copy-start.3 = (bf16[1,8,2,16,512]{4,3,2,1,0:T(8,128)(2,1)S(1)}, bf16[1,8,2,16,512]{4,3,2,1,0:T(8,128)(2,1)}, u32[]{:S(2)}) copy-start(bf16[1,8,2,16,512]{4,3,2,1,0:T(8,128)(2,1)} %param.4) | copy-start | bytes 786436
  2.0 17.6 %collective-permute-start.11 = (s32[1,1]{1,0:T(1,128)}, s32[1,1]{1,0:T(1,128)}, u32[]{:S(2)}, u32[]{:S(2)}) collective-permute-start(s32[1,1]{1,0:T(1,128)} %get-tuple-element.29), channel_id=1, source_target_pairs={{2,0},{4,2},{6,4},{3,1},{5,3},{7,5},{10,8},{12,10},{14,12},{11,9},... | collective-permute-start | bytes 20 | tf_op jit(solution)/shard_map/ppermute | solution.py:26
  4.1 17.1 %collective-permute-start.5 = (s32[1,1]{1,0:T(1,128)}, s32[1,1]{1,0:T(1,128)}, u32[]{:S(2)}, u32[]{:S(2)}) collective-permute-start(s32[1,1]{1,0:T(1,128)} %get-tuple-element.30), channel_id=1, source_target_pairs={{0,2},{2,4},{4,6},{1,3},{3,5},{5,7},{8,10},{10,12},{12,14},{9,11},... | collective-permute-start | bytes 20 | tf_op jit(solution)/shard_map/ppermute | solution.py:26
  8.9 23.7 %collective-permute-start = (bf16[1,2,1,16,512]{4,3,2,1,0:T(8,128)(2,1)S(1)}, bf16[1,2,1,16,512]{4,3,2,1,0:T(8,128)(2,1)S(1)}, u32[]{:S(2)}, u32[]{:S(2)}) collective-permute-start(bf16[1,2,1,16,512]{4,3,2,1,0:T(8,128)(2,1)S(1)} %get-tuple-element.17), channel_id=1, source_target_pairs={{0,3},{2,5},{4,7},{8,11},{10,13},{12,15},{16,19},{18,21},{20,23},{... | collective-permute-start | bytes 98312 | tf_op jit(solution)/shard_map/ppermute | solution.py:38
  10.2 22.4 %collective-permute-start.2 = (bf16[1,2,1,16,512]{4,3,2,1,0:T(8,128)(2,1)S(1)}, bf16[1,2,1,16,512]{4,3,2,1,0:T(8,128)(2,1)S(1)}, u32[]{:S(2)}, u32[]{:S(2)}) collective-permute-start(bf16[1,2,1,16,512]{4,3,2,1,0:T(8,128)(2,1)S(1)} %get-tuple-element.18), channel_id=1, source_target_pairs={{1,2},{3,4},{5,6},{9,10},{11,12},{13,14},{17,18},{19,20},{21,22},{... | collective-permute-start | bytes 98312 | tf_op jit(solution)/shard_map/ppermute | solution.py:38
  14.9 17.7 %collective-permute-start.1 = (bf16[1,2,2,16,512]{4,3,2,1,0:T(8,128)(2,1)S(1)}, bf16[1,2,2,16,512]{4,3,2,1,0:T(8,128)(2,1)S(1)}, u32[]{:S(2)}, u32[]{:S(2)}) collective-permute-start(bf16[1,2,2,16,512]{4,3,2,1,0:T(8,128)(2,1)S(1)} %slice.65), channel_id=1, source_target_pairs={{0,2},{2,4},{4,6},{1,3},{3,5},{5,7},{8,10},{10,12},{12,14},{9,11},... | collective-permute-start | bytes 196616 | tf_op jit(solution)/shard_map/ppermute | solution.py:26
  19.6 13.0 %collective-permute-start.4 = (bf16[1,8,1,16,512]{4,3,2,1,0:T(8,128)(2,1)S(1)}, bf16[1,8,1,16,512]{4,3,2,1,0:T(8,128)(2,1)S(1)}, u32[]{:S(2)}, u32[]{:S(2)}) collective-permute-start(bf16[1,8,1,16,512]{4,3,2,1,0:T(8,128)(2,1)S(1)} %get-tuple-element.19), channel_id=1, source_target_pairs={{1,0},{3,2},{5,4},{7,6},{9,8},{11,10},{13,12},{15,14},{17,16},{19,... | collective-permute-start | bytes 393224 | tf_op jit(solution)/shard_map/ppermute | solution.py:19
  21.3 11.2 %collective-permute-start.3 = (bf16[1,8,1,16,512]{4,3,2,1,0:T(8,128)(2,1)S(1)}, bf16[1,8,1,16,512]{4,3,2,1,0:T(8,128)(2,1)S(1)}, u32[]{:S(2)}, u32[]{:S(2)}) collective-permute-start(bf16[1,8,1,16,512]{4,3,2,1,0:T(8,128)(2,1)S(1)} %get-tuple-element.20), channel_id=1, source_target_pairs={{0,1},{2,3},{4,5},{6,7},{8,9},{10,11},{12,13},{14,15},{16,17},{18,... | collective-permute-start | bytes 393224 | tf_op jit(solution)/shard_map/ppermute | solution.py:18
  24.5 8.4 %copy-start = (bf16[1,4,2,16,512]{4,3,2,1,0:T(8,128)(2,1)S(1)}, bf16[1,4,2,16,512]{4,3,2,1,0:T(8,128)(2,1)}, u32[]{:S(2)}) copy-start(bf16[1,4,2,16,512]{4,3,2,1,0:T(8,128)(2,1)} %param.7) | copy-start | bytes 393220
  26.6 69.9 %all-to-all-start = ((bf16[32,16,384]{2,1,0:T(8,128)(2,1)}), bf16[32,16,384]{2,1,0:T(8,128)(2,1)S(1)}, u32[]{:S(2)}, u32[]{:S(2)}) async-start(bf16[32,16,384]{2,1,0:T(8,128)(2,1)} %bitcast.22), calls=%async_computation | async-start | bytes 786432 | tf_op jit(solution)/shard_map/all_to_all | solution.py:282
  43.1 9.4 %collective-permute-start.8 = (bf16[1,1,1,16,512]{4,3,2,1,0:T(8,128)(2,1)S(1)}, bf16[1,1,1,16,512]{4,3,2,1,0:T(8,128)(2,1)S(1)}, u32[]{:S(2)}, u32[]{:S(2)}) collective-permute-start(bf16[1,1,1,16,512]{4,3,2,1,0:T(8,128)(2,1)S(1)} %get-tuple-element.21), channel_id=1, source_target_pairs={{2,1},{4,3},{6,5},{10,9},{12,11},{14,13},{18,17},{20,19},{22,21},{... | collective-permute-start | bytes 49160 | tf_op jit(solution)/shard_map/ppermute | solution.py:38
  44.4 8.1 %collective-permute-start.10 = (bf16[1,1,1,16,512]{4,3,2,1,0:T(8,128)(2,1)S(1)}, bf16[1,1,1,16,512]{4,3,2,1,0:T(8,128)(2,1)S(1)}, u32[]{:S(2)}, u32[]{:S(2)}) collective-permute-start(bf16[1,1,1,16,512]{4,3,2,1,0:T(8,128)(2,1)S(1)} %get-tuple-element.22), channel_id=1, source_target_pairs={{3,0},{5,2},{7,4},{11,8},{13,10},{15,12},{19,16},{21,18},{23,20},{... | collective-permute-start | bytes 49160 | tf_op jit(solution)/shard_map/ppermute | solution.py:38
  46.2 7.4 %collective-permute-start.9 = (bf16[1,1,2,16,512]{4,3,2,1,0:T(8,128)(2,1)S(1)}, bf16[1,1,2,16,512]{4,3,2,1,0:T(8,128)(2,1)S(1)}, u32[]{:S(2)}, u32[]{:S(2)}) collective-permute-start(bf16[1,1,2,16,512]{4,3,2,1,0:T(8,128)(2,1)S(1)} %slice.88), channel_id=1, source_target_pairs={{2,0},{4,2},{6,4},{3,1},{5,3},{7,5},{10,8},{12,10},{14,12},{11,9},... | collective-permute-start | bytes 98312 | tf_op jit(solution)/shard_map/ppermute | solution.py:26
  48.1 5.5 %collective-permute-start.6 = (bf16[1,4,1,16,512]{4,3,2,1,0:T(8,128)(2,1)S(1)}, bf16[1,4,1,16,512]{4,3,2,1,0:T(8,128)(2,1)S(1)}, u32[]{:S(2)}, u32[]{:S(2)}) collective-permute-start(bf16[1,4,1,16,512]{4,3,2,1,0:T(8,128)(2,1)S(1)} %get-tuple-element.23), channel_id=1, source_target_pairs={{0,1},{2,3},{4,5},{6,7},{8,9},{10,11},{12,13},{14,15},{16,17},{18,... | collective-permute-start | bytes 196616 | tf_op jit(solution)/shard_map/ppermute | solution.py:18
  49.4 4.2 %collective-permute-start.7 = (bf16[1,4,1,16,512]{4,3,2,1,0:T(8,128)(2,1)S(1)}, bf16[1,4,1,16,512]{4,3,2,1,0:T(8,128)(2,1)S(1)}, u32[]{:S(2)}, u32[]{:S(2)}) collective-permute-start(bf16[1,4,1,16,512]{4,3,2,1,0:T(8,128)(2,1)S(1)} %get-tuple-element.24), channel_id=1, source_target_pairs={{1,0},{3,2},{5,4},{7,6},{9,8},{11,10},{13,12},{15,14},{17,16},{19,... | collective-permute-start | bytes 196616 | tf_op jit(solution)/shard_map/ppermute | solution.py:19
  94.6 2.0 %copy-start.1 = (bf16[32,128,512]{2,1,0:T(8,128)(2,1)}, bf16[32,128,512]{2,1,0:T(8,128)(2,1)S(1)}, u32[]{:S(2)}) copy-start(bf16[32,128,512]{2,1,0:T(8,128)(2,1)S(1)} %get-tuple-element.10) | copy-start | bytes 12582916
  105.9 2.2 %copy-start.2 = (bf16[32,128,512]{2,1,0:T(8,128)(2,1)S(1)}, bf16[32,128,512]{2,1,0:T(8,128)(2,1)}, u32[]{:S(2)}) copy-start(bf16[32,128,512]{2,1,0:T(8,128)(2,1)} %copy-done.1) | copy-start | bytes 12582916
